TPU v7x, 512 devices: a whole 4x8x8 slice. The times are simulated.
512 devices in a mesh: cuts: 32 (over x, y), col: 16 (over z, core).
Axes of the slice: x: 4, y: 8, z: 8, core: 2. Of those that a mesh axis runs over, the one named last changes fastest.
Arguments:
- levels: int32 [64, 1024], P('cuts'), may hold values from 0 to 65535
- start_basis: float32 [32, 1024, 2048], P('cuts', 'col'), may hold values from -6 to 6
Outputs:
- exponents: float32 [1024], P('col')
- running_means: float32 [1024], P('col')
- handed: float32 [32, 1024, 2048], P('cuts', 'col')
All inputs are finite; a program needn't handle non-finite values.
Results may differ from a plain program's by a relative error of at most 0.0009.
Values sent between devices are 32-bit elements; how exact they have to be, the bound alone decides.
A program may use at most 64 MiB of HBM per device.

v0:
```python
import math

import jax
import jax.numpy as jnp
from jax import lax
from jax.sharding import PartitionSpec as P

M = 32
K = 1024
SLICES = 2
SITES = 1024
ROWS = 2048


energy = 0.5
disorder = 4.0
level_span = 65536.0


def from_behind(block, axis, distance):
    devices = range(lax.axis_size(axis))
    route = [(i - distance, i) for i in devices if i - distance in devices]
    return lax.ppermute(block, axis, route)


def neighbours(signal):
    grid = signal.reshape(signal.shape[:-1] + (M, M))
    summed = (
        jnp.roll(grid, 1, -1)
        + jnp.roll(grid, -1, -1)
        + jnp.roll(grid, 1, -2)
        + jnp.roll(grid, -1, -2)
    )
    return summed.reshape(signal.shape)


def local(levels, start_basis):
    seg_start = start_basis[0]
    block_width = seg_start.shape[0]
    upper = seg_start[:, :SITES]
    lower = seg_start[:, SITES:]
    for sweep_index in range(SLICES):
        onsite = disorder * (levels[sweep_index].astype(jnp.float32) / level_span - 0.5)
        advanced = (energy - onsite) * upper - neighbours(upper) - lower
        lower = upper
        upper = advanced
    propagated = jnp.concatenate([upper, lower], axis=1)
    contract = (((1,), (1,)), ((), ()))
    spread = lax.all_to_all(propagated, "col", split_axis=1, concat_axis=0, tiled=True)
    product = lax.dot_general(
        propagated,
        lax.all_gather(propagated, "col", axis=0, tiled=True),
        contract,
        precision=lax.Precision.HIGHEST,
        preferred_element_type=jnp.float32,
    )
    gram_matrix = lax.all_gather(product, "col", axis=0, tiled=True)
    factor = jnp.linalg.cholesky(gram_matrix)
    log_pivots = jnp.log(jnp.diagonal(factor)) - 0.5 * math.log(ROWS)
    row_part = jax.scipy.linalg.solve_triangular(factor, spread, lower=True) * math.sqrt(ROWS)
    own_basis = lax.all_to_all(row_part, "col", split_axis=0, concat_axis=1, tiled=True)
    arriving = from_behind(own_basis, "cuts", 1)
    first_cut = lax.axis_index("cuts") == 0
    handed = jnp.where(first_cut, seg_start, arriving)[None]
    position = lax.axis_index("col")
    segments = SLICES * lax.axis_size("cuts")
    summed = lax.psum(log_pivots, "cuts")
    all_exponents = summed / segments
    counts_all = jnp.arange(1, K + 1).astype(jnp.float32)
    all_running = jnp.cumsum(all_exponents) / counts_all
    exponents = lax.dynamic_slice_in_dim(all_exponents, position * block_width, block_width)
    running_means = lax.dynamic_slice_in_dim(all_running, position * block_width, block_width)
    return (exponents, running_means, handed)


def solution(mesh):
    in_specs = (P("cuts", None), P("cuts", "col", None))
    out_specs = (P("col"), P("col"), P("cuts", "col", None))
    return jax.shard_map(local, mesh=mesh, in_specs=in_specs, out_specs=out_specs, check_vma=False)
```

profile of v0, /device:TPU:8, one launch (start us, length us, event | category | flops | bytes accessed | tf_op | source)
XLA Modules:
  0.0 587.1 jit_solution(8906127877331775109)
XLA Ops:
  7.2 1.4 copy.14
  10.3 1.1 copy.15
  11.5 64.0 %all-gather.3.cloned.1.call-done = f32[1024,2048]{1,0:T(8,128)} async-done(((f32[64,2048]{1,0:T(8,128)}), f32[1024,2048]{1,0:T(8,128)}) %all-gather.3.cloned.1.call-update) | async-done | bytes 8388624 | tf_op jit(solution)/shard_map/all_gather | solution.py:52
  75.5 11.3 %fusion.67 = f32[64,1024]{1,0:T(8,128)} fusion(f32[1024,2048]{1,0:T(8,128)} %all-gather.3.cloned.1.call-done, f32[64,1024]{0,1:T(8,128)S(1)} %slice_subtract_fusion, f32[64,1024]{0,1:T(8,128)S(1)} %fusion.11), kind=kOutput, calls=%fused_computation.177 | convolution fusion | flops 1610743808 | bytes 9175040 | tf_op jit(solution)/shard_map/dot_general | solution.py:50
  86.8 1.1 copy.17
  87.9 4.2 all-to-all-start
  92.1 17.6 %all-to-all-done = f32[64,16,128]{2,0,1:T(8,128)S(1)} async-done(((f32[64,16,128]{2,0,1:T(8,128)}), f32[64,16,128]{2,0,1:T(8,128)S(1)}, u32[]{:S(2)}, u32[]{:S(2)}) %all-to-all-start) | async-done | bytes 524320 | tf_op jit(solution)/shard_map/all_to_all | solution.py:49
  109.7 25.1 %all-gather.5.cloned.1.call-done = f32[1024,1024]{1,0:T(8,128)} async-done(((f32[64,1024]{1,0:T(8,128)}), f32[1024,1024]{1,0:T(8,128)}) %all-gather.5.cloned.1.call-update) | async-done | bytes 4194320 | tf_op jit(solution)/shard_map/all_gather | solution.py:57
  134.8 5.8 copy.16
  140.7 4.4 fusion
  145.1 1.9 copy-done
  147.0 11.7 %cholesky.223 = f32[128,128]{1,0:T(8,128)S(1)} custom-call(f32[128,128]{1,0:T(8,128)S(1)} %cholesky.580), custom_call_target="Cholesky" | custom-call | tf_op jit(solution)/shard_map/jit(cholesky)/cholesky | solution.py:58
  158.8 2.5 cholesky.255
  161.3 9.8 %custom-call.63 = f32[1,128,128]{1,2,0:T(8,128)S(1)} custom-call(f32[1,128,128]{2,1,0:T(8,128)S(1)} %get-tuple-element.99), custom_call_target="InvertDiagBlocksLowerTriangular" | custom-call | tf_op jit(solution)/shard_map/jit(cholesky)/cholesky | solution.py:58
  171.1 2.3 constant_dynamic-update-slice_fusion.32
  173.5 1.5 convolution_subtract_fusion
  175.0 11.9 %cholesky.244 = f32[128,128]{1,0:T(8,128)S(1)} custom-call(f32[128,128]{1,0:T(8,128)S(1)} %cholesky.584), custom_call_target="Cholesky" | custom-call | tf_op jit(solution)/shard_map/jit(cholesky)/cholesky | solution.py:58
  187.5 9.8 %custom-call.64 = f32[1,128,128]{1,2,0:T(8,128)S(1)} custom-call(f32[1,128,128]{2,1,0:T(8,128)S(1)} %get-tuple-element.96), custom_call_target="InvertDiagBlocksLowerTriangular" | custom-call | tf_op jit(solution)/shard_map/jit(cholesky)/cholesky | solution.py:58
  197.3 1.2 convolution_dynamic-update-slice_fusion
  198.6 2.1 convolution_subtract_fusion.1
  200.7 11.7 %cholesky.468 = f32[128,128]{1,0:T(8,128)S(1)} custom-call(f32[128,128]{1,0:T(8,128)S(1)} %cholesky.589), custom_call_target="Cholesky" | custom-call | tf_op jit(solution)/shard_map/jit(cholesky)/cholesky | solution.py:58
  213.7 9.8 %custom-call.65 = f32[1,128,128]{1,2,0:T(8,128)S(1)} custom-call(f32[1,128,128]{2,1,0:T(8,128)S(1)} %get-tuple-element.93), custom_call_target="InvertDiagBlocksLowerTriangular" | custom-call | tf_op jit(solution)/shard_map/jit(cholesky)/cholesky | solution.py:58
  223.5 1.2 convolution_dynamic-update-slice_fusion.1
  224.7 2.3 convolution_subtract_fusion.2
  227.0 11.9 %cholesky.487 = f32[128,128]{1,0:T(8,128)S(1)} custom-call(f32[128,128]{1,0:T(8,128)S(1)} %cholesky.594), custom_call_target="Cholesky" | custom-call | tf_op jit(solution)/shard_map/jit(cholesky)/cholesky | solution.py:58
  240.2 9.8 %custom-call.66 = f32[1,128,128]{1,2,0:T(8,128)S(1)} custom-call(f32[1,128,128]{2,1,0:T(8,128)S(1)} %get-tuple-element.90), custom_call_target="InvertDiagBlocksLowerTriangular" | custom-call | tf_op jit(solution)/shard_map/jit(cholesky)/cholesky | solution.py:58
  250.0 1.1 convolution_dynamic-update-slice_fusion.2
  251.1 2.3 convolution_subtract_fusion.3
  253.5 11.7 %cholesky.506 = f32[128,128]{1,0:T(8,128)S(1)} custom-call(f32[128,128]{1,0:T(8,128)S(1)} %cholesky.599), custom_call_target="Cholesky" | custom-call | tf_op jit(solution)/shard_map/jit(cholesky)/cholesky | solution.py:58
  266.5 10.2 %custom-call.67 = f32[1,128,128]{1,2,0:T(8,128)S(1)} custom-call(f32[1,128,128]{2,1,0:T(8,128)S(1)} %get-tuple-element.87), custom_call_target="InvertDiagBlocksLowerTriangular" | custom-call | tf_op jit(solution)/shard_map/jit(cholesky)/cholesky | solution.py:58
  276.7 1.0 convolution_dynamic-update-slice_fusion.3
  277.7 2.3 convolution_subtract_fusion.4
  280.0 11.7 %cholesky.526 = f32[128,128]{1,0:T(8,128)S(1)} custom-call(f32[128,128]{1,0:T(8,128)S(1)} %cholesky.604), custom_call_target="Cholesky" | custom-call | tf_op jit(solution)/shard_map/jit(cholesky)/cholesky | solution.py:58
  293.1 9.8 %custom-call.68 = f32[1,128,128]{1,2,0:T(8,128)S(1)} custom-call(f32[1,128,128]{2,1,0:T(8,128)S(1)} %get-tuple-element.84), custom_call_target="InvertDiagBlocksLowerTriangular" | custom-call | tf_op jit(solution)/shard_map/jit(cholesky)/cholesky | solution.py:58
  303.9 2.0 convolution_subtract_fusion.5
  305.9 11.9 %cholesky.546 = f32[128,128]{1,0:T(8,128)S(1)} custom-call(f32[128,128]{1,0:T(8,128)S(1)} %cholesky.609), custom_call_target="Cholesky" | custom-call | tf_op jit(solution)/shard_map/jit(cholesky)/cholesky | solution.py:58
  319.0 9.8 %custom-call.69 = f32[1,128,128]{1,2,0:T(8,128)S(1)} custom-call(f32[1,128,128]{2,1,0:T(8,128)S(1)} %get-tuple-element.81), custom_call_target="InvertDiagBlocksLowerTriangular" | custom-call | tf_op jit(solution)/shard_map/jit(cholesky)/cholesky | solution.py:58
  329.7 1.8 convolution_subtract_fusion.11
  331.5 11.7 %cholesky.564 = f32[128,128]{1,0:T(8,128)S(1)} custom-call(f32[128,128]{1,0:T(8,128)S(1)} %convolution_subtract_fusion.11), custom_call_target="Cholesky" | custom-call | tf_op jit(solution)/shard_map/jit(cholesky)/cholesky | solution.py:58
  350.1 6.6 %fusion.1 = (f32[1024,1024]{1,0:T(8,128)}, f32[1024,1024]{1,0:T(8,128)}) fusion(f32[1024,1024]{1,0:T(8,128)} %get-tuple-element.79, pred[]{:T(512)S(6)} %cholesky.579), kind=kLoop, calls=%fused_computation.7 | loop fusion | flops 4194304 | bytes 12582913 | tf_op jit(solution)/shard_map/jit(_solve_triangular)/triangular_solve | solution.py:60
  356.7 23.2 %while.1 = (s32[]{:T(128)}, f32[1024,1024]{1,0:T(8,128)}, s32[8,2]{0,1:T(2,128)S(1)}, f32[8,128,128]{2,1,0:T(8,128)S(1)}, s32[]{:T(128)}) while((s32[]{:T(128)}, f32[1024,1024]{1,0:T(8,128)}, s32[8,2]{0,1:T(2,128)S(1)}, f32[8,128,128]{2,1,0:T(8,128)S(1)}, s32[]{:T(128)}) %tuple.81), condition=%wide.while_cond, body=%wide.while_body.sunk | while | flops 2 | bytes 131181 | solution.py:60
  357.3 2.3 bitcast_dynamic-update-slice_fusion.2
  360.2 2.3 bitcast_dynamic-update-slice_fusion.2
  363.1 2.3 bitcast_dynamic-update-slice_fusion.2
  366.0 2.3 bitcast_dynamic-update-slice_fusion.2
  368.9 2.3 bitcast_dynamic-update-slice_fusion.2
  371.8 2.3 bitcast_dynamic-update-slice_fusion.2
  374.7 2.3 bitcast_dynamic-update-slice_fusion.2
  377.6 2.2 bitcast_dynamic-update-slice_fusion.2
  379.9 78.8 %custom-call.70 = f32[8,128,128]{1,2,0:T(8,128)S(1)} custom-call(f32[8,128,128]{2,1,0:T(8,128)S(1)} %get-tuple-element.10), custom_call_target="InvertDiagBlocksLowerTriangular" | custom-call | tf_op jit(solution)/shard_map/jit(_solve_triangular)/triangular_solve | solution.py:60
  459.0 1.0 convolution_subtract_fusion.10
  460.3 1.2 convolution_subtract_fusion.9
  461.8 1.2 convolution_subtract_fusion.13
  463.3 1.3 convolution_subtract_fusion.12
  465.0 1.4 convolution_subtract_fusion.8
  466.7 1.5 convolution_subtract_fusion.7
  468.5 1.6 convolution_subtract_fusion.6
  471.2 4.6 all-to-all-start.1
  475.8 16.8 %gather_fusion = f32[1024]{0:T(1024)S(1)} fusion(f32[1024,1024]{1,0:T(8,128)} %get-tuple-element.26, s32[1024]{0:T(1024)S(1)} %bitcast.141), kind=kCustom, calls=%fused_computation | custom fusion | bytes 16384 | tf_op jit(solution)/shard_map/jit(diagonal)/cond/branch_0_fun/gather | solution.py:59
  492.7 71.2 %psum.7 = f32[1024]{0:T(1024)S(1)} all-reduce(f32[1024]{0:T(1024)S(1)} %log_add_fusion), channel_id=1, replica_groups=mesh['cuts'=32,'col'=16] {'cuts'}, use_global_device_ids=true, to_apply=%region_16.17 | all-reduce | flops 1024 | bytes 8192 | tf_op jit(solution)/shard_map/psum | solution.py:67
  563.9 2.6 collective-permute-start
  568.3 8.0 %collective-permute-done = f32[64,2048]{1,0:T(8,128)S(1)} collective-permute-done((f32[64,2048]{1,0:T(8,128)S(1)}, f32[64,2048]{1,0:T(8,128)S(1)}, u32[]{:S(2)}, u32[]{:S(2)}) %collective-permute-start) | collective-permute-done | bytes 524320 | tf_op jit(solution)/shard_map/ppermute | solution.py:23
  576.6 1.1 select_bitcast_fusion
  577.7 2.3 copy.20
  (88 shorter events, 22.7 us)
Async XLA Ops:
  7.2 1.8 copy-start.1
  7.2 68.3 %all-gather.3.cloned.1.call-start = ((), (), s32[]{:S(2)}) async-start(), calls=%async_computation.2 | async-start | bytes 8912896 | tf_op jit(solution)/shard_map/all_gather | solution.py:52
  11.4 123.4 %all-gather.5.cloned.1.call-start = ((), (), s32[]{:S(2)}) async-start(), calls=%async_computation.3 | async-start | bytes 4456448 | tf_op jit(solution)/shard_map/all_gather | solution.py:57
  87.9 21.8 %all-to-all-start = ((f32[64,16,128]{2,0,1:T(8,128)}), f32[64,16,128]{2,0,1:T(8,128)S(1)}, u32[]{:S(2)}, u32[]{:S(2)}) async-start(f32[64,16,128]{2,0,1:T(8,128)} %copy.17), calls=%async_computation | async-start | bytes 1048576 | tf_op jit(solution)/shard_map/all_to_all | solution.py:49
  145.1 1.9 copy-start
  471.2 92.7 %all-to-all-start.1 = ((f32[16,64,128]{2,1,0:T(8,128)}), f32[16,64,128]{2,1,0:T(8,128)S(1)}, u32[]{:S(2)}, u32[]{:S(2)}) async-start(f32[16,64,128]{2,1,0:T(8,128)} %bitcast.43), calls=%async_computation.1 | async-start | bytes 1048576 | tf_op jit(solution)/shard_map/all_to_all | solution.py:61
  563.9 12.3 %collective-permute-start = (f32[64,2048]{1,0:T(8,128)S(1)}, f32[64,2048]{1,0:T(8,128)S(1)}, u32[]{:S(2)}, u32[]{:S(2)}) collective-permute-start(f32[64,2048]{1,0:T(8,128)S(1)} %copy_bitcast_fusion), channel_id=1, source_target_pairs={{0,16},{16,32},{32,48},{48,64},{64,80},{80,96},{96,112},{112,128},... | collective-permute-start | bytes 1572872 | tf_op jit(solution)/shard_map/ppermute | solution.py:23
Sparse Core Ops, SparseCore 0:
  11.5 63.9 all-gather.2
  86.9 47.8 all-gather.4
where the time goes:
time: 594 us; the launch traced here: 587 us
  other arithmetic  265 us (45%)
  waiting for transfers between devices  115 us (19%)
  blocking collectives  71.2 us (12%)
  local copies, waits for them, and re-layouts  58.4 us (10%)
  matrix products  45.9 us (8%)
  between operations  19.8 us (3%)
  starting transfers between devices  11.4 us (2%)
    another operation x30, other arithmetic, local(): factor = jnp.linalg.cholesky(gram_matrix)  172 us
    another operation x3, other arithmetic, local(): jax.scipy.linalg.solve_triangular(factor, spread, lower=True)  85.4 us
    psum x1, blocking collectives, local(): summed = lax.psum(log_pivots, 'cuts')  71.2 us
    all_gather x1, waiting for transfers between devices, local(): lax.all_gather(propagated, 'col', axis=0, tiled=True)  64 us
    all_gather x1, waiting for transfers between devices, local(): gram_matrix = lax.all_gather(product, 'col', axis=0, tiled=True)  25.1 us
    another operation x26, local copies, waits for them, and re-layouts  23.2 us
    another operation x14, matrix products, local(): factor = jnp.linalg.cholesky(gram_matrix)  23.1 us
    all_to_all x1, waiting for transfers between devices, local(): lax.all_to_all(propagated, 'col', split_axis=1, concat_axis=0, tiled=True)  17.6 us
  transfers between devices with their start and end apart: 5, of which 4 were waited for; matrix products, arithmetic and copies ran while one was open for 3% of the time, Pallas kernels for 0%

commit v1 on v0

v1 whole, which is shorter than its diff:
```python
import functools
import math

import jax
import jax.numpy as jnp
from jax import lax
from jax.experimental import pallas as pl
from jax.experimental.pallas import tpu as pltpu
from jax.sharding import PartitionSpec as P

M = 32
SITES = 1024
ROWS = 2048
SLICES = 2
B = 128
HALF = 64
CHIPS = 8
COL = 16
K = 1024
BANDS = 5 * B

energy = 0.5
disorder = 4.0
level_span = 65536.0

MESH = pl.DeviceIdType.MESH
VMEM = pl.BlockSpec(memory_space=pltpu.VMEM)
f32 = jnp.float32


def dot(a, b, ca, cb):
    return lax.dot_general(
        a, b, (((ca,), (cb,)), ((), ())), precision=lax.Precision.HIGHEST, preferred_element_type=f32
    )


def remote(src, dst, send, recv, device):
    return pltpu.make_async_remote_copy(
        src_ref=src, dst_ref=dst, send_sem=send, recv_sem=recv, device_id=device, device_id_type=MESH
    )


def neighbours(x):
    site = lax.broadcasted_iota(jnp.int32, x.shape, 1)
    b = lax.rem(site, M)
    around = lambda by: pltpu.roll(x, by % SITES, 1)
    along = jnp.where(b == 0, around(1 - M), around(1)) + jnp.where(b == M - 1, around(M - 1), around(-1))
    return along + around(M) + around(-M)


def gram_kernel(
    lev, start, slab, gall, prop, gat, part, other,
    gs, gr, fs, als, alr, ps, pr, ags, agr, ins, inr,
):
    me = lax.axis_index("col")
    z, h = me // 2, me % 2
    up, down = lax.rem(z + 1, CHIPS), lax.rem(z + CHIPS - 1, CHIPS)
    partner = z * 2 + 1 - h
    mine = pl.ds(pl.multiple_of(h * HALF, HALF), HALF)
    theirs = pl.ds(pl.multiple_of((1 - h) * HALF, HALF), HALF)

    barrier = pltpu.get_barrier_semaphore()
    for o in range(1, COL):
        pl.semaphore_signal(barrier, inc=1, device_id={"col": lax.rem(me + o, COL)}, device_id_type=MESH)

    upper = start[:, :SITES]
    lower = start[:, SITES:]
    for n in range(SLICES):
        onsite = disorder * (lev[n : n + 1, :].astype(f32) / level_span - 0.5)
        upper, lower = (energy - onsite) * upper - neighbours(upper) - lower, upper
    prop[:, :SITES] = upper
    prop[:, SITES:] = lower
    pl.semaphore_wait(barrier, COL - 1)

    halves = [prop.at[:, pl.ds(g * SITES, SITES)] for g in range(2)]
    sends = []
    for g in range(2):
        sends.append(remote(halves[g], gat.at[1, mine], gs.at[g], gr.at[2 + h], {"col": up * 2 + g}))
        sends.append(remote(halves[g], gat.at[3, mine], gs.at[2 + g], gr.at[6 + h], {"col": down * 2 + g}))
    for s in sends:
        s.start()
    own_half = pl.ds(pl.multiple_of(h * SITES, SITES), SITES)
    their_half = pl.ds(pl.multiple_of((1 - h) * SITES, SITES), SITES)
    swap = remote(prop.at[:, their_half], gat.at[0, mine], gs.at[4], gr.at[h], {"col": partner})
    swap.start()
    sends.append(swap)
    gat[0, mine, :] = prop[:, own_half]

    def arrived(slot, s):
        rows = pl.ds(s * HALF, HALF)
        remote(gat.at[slot, rows], gat.at[slot, rows], gs.at[0], gr.at[2 * slot + s], {"col": partner}).wait_recv()

    for s in range(2):
        rows = pl.ds(s * HALF, HALF)
        arrived(1, s)
        f = remote(gat.at[1, rows], gat.at[2, rows], fs.at[s], gr.at[4 + s], {"col": up * 2 + h})
        f.start()
        sends.append(f)
        arrived(3, s)
        f = remote(gat.at[3, rows], gat.at[4, rows], fs.at[2 + s], gr.at[8 + s], {"col": down * 2 + h})
        f.start()
        sends.append(f)

    my_rows = pl.ds(pl.multiple_of(me * HALF, HALF), HALF)
    for o in range(1, COL):
        d = lax.rem(me + o, COL)
        s = remote(
            prop.at[:, pl.ds(pl.multiple_of(d * B, B), B)], slab.at[my_rows], als.at[o], alr.at[o], {"col": d}
        )
        s.start()
        sends.append(s)
    slab[my_rows, :] = prop[:, pl.ds(pl.multiple_of(me * B, B), B)]

    remote(gat.at[0, theirs], gat.at[0, theirs], gs.at[0], gr.at[1 - h], {"col": partner}).wait_recv()
    part[:, 0:B] = dot(gat[0], gat[0], 1, 1)
    part[:, B : 2 * B] = dot(gat[0], gat[3], 1, 1)
    for s in range(2):
        arrived(2, s)
        arrived(4, s)
    part[:, 2 * B : 3 * B] = dot(gat[0], gat[4], 1, 1)
    part[:, 3 * B : 4 * B] = dot(gat[1], gat[4], 1, 1)
    part[:, 4 * B : 5 * B] = dot(gat[2], gat[4], 1, 1)

    both = remote(part.at[theirs], other, ps, pr, {"col": partner})
    both.start()
    both.wait_recv()
    sends.append(both)
    gall[z, mine, :] = part[mine, :] + other[...]

    def inside(chip, rows, i):
        s = remote(gall.at[chip, rows], gall.at[chip, rows], ins.at[i], inr.at[i], {"col": partner})
        s.start()
        sends.append(s)

    quarter = HALF // 2
    first = pl.ds(pl.multiple_of(h * HALF, quarter), quarter)
    second = pl.ds(pl.multiple_of(h * HALF + quarter, quarter), quarter)
    for d in range(1, 5):
        behind, ahead = lax.rem(z + CHIPS - d, CHIPS), lax.rem(z + d, CHIPS)
        cw_chip, cc_chip = lax.rem(z + CHIPS - d + 1, CHIPS), lax.rem(z + d - 1, CHIPS)
        cw_rows, cc_rows = (mine, mine) if d < 4 else (first, second)
        cw = remote(
            gall.at[cw_chip, cw_rows], gall.at[cw_chip, cw_rows], ags.at[d], agr.at[d], {"col": up * 2 + h}
        )
        cc = remote(
            gall.at[cc_chip, cc_rows], gall.at[cc_chip, cc_rows], ags.at[4 + d], agr.at[4 + d], {"col": down * 2 + h}
        )
        cw.start()
        cc.start()
        if d == 1:
            inside(z, mine, 0)
        sends += [cw, cc]
        remote(gall.at[behind, cw_rows], gall.at[behind, cw_rows], gs.at[0], agr.at[d], {"col": partner}).wait_recv()
        inside(behind, cw_rows, d)
        remote(gall.at[ahead, cc_rows], gall.at[ahead, cc_rows], gs.at[0], agr.at[4 + d], {"col": partner}).wait_recv()
        inside(ahead, cc_rows, 4 + d)

    t_first = pl.ds(pl.multiple_of((1 - h) * HALF, quarter), quarter)
    t_second = pl.ds(pl.multiple_of((1 - h) * HALF + quarter, quarter), quarter)
    for d in range(0, 5):
        behind, ahead = lax.rem(z + CHIPS - d, CHIPS), lax.rem(z + d, CHIPS)
        cw_rows, cc_rows = (theirs, theirs) if d < 4 else (t_first, t_second)
        remote(gall.at[behind, cw_rows], gall.at[behind, cw_rows], gs.at[0], inr.at[d], {"col": partner}).wait_recv()
        if d:
            remote(gall.at[ahead, cc_rows], gall.at[ahead, cc_rows], gs.at[0], inr.at[4 + d], {"col": partner}).wait_recv()
    for o in range(1, COL):
        rows = pl.ds(pl.multiple_of(lax.rem(me + COL - o, COL) * HALF, HALF), HALF)
        remote(slab.at[rows], slab.at[rows], gs.at[0], alr.at[o], {"col": partner}).wait_recv()
    for s in sends:
        s.wait_send()


def eliminate(d, out):
    tiles = [d[8 * t : 8 * t + 8, :] for t in range(B // 8)]
    last = len(tiles) - 1
    lane = lax.broadcasted_iota(jnp.int32, (8, B), 1)
    row = lambda v, i: jnp.broadcast_to(v[i : i + 1, :], (8, B))
    col = lambda v, c: jnp.broadcast_to(v[:, c : c + 1], (8, B))
    for q, tile in enumerate(tiles):
        tile = tiles[q]
        c0 = 8 * q
        rows = [row(tile, j) for j in range(8)]
        a = {(m, j): col(rows[m], c0 + j) for m in range(8) for j in range(m, 8)}
        block = jnp.logical_and(lane >= c0, lane < c0 + 8)
        e = [jnp.where(block, jnp.where(lane == c0 + j, 1.0, 0.0), rows[j]) for j in range(8)]
        f0, f1, w = {}, {}, [None] * 8
        for i in range(0, 8, 2):
            k = i + 1
            p, r, s = a[i, i], a[i, k], a[k, k]
            over = 1.0 / (p * s - r * r)
            for j in range(k + 1, 8):
                x, y = a[i, j], a[k, j]
                f0[i, j] = (s * x - r * y) * over
                f1[i, j] = (p * y - r * x) * over
                for m in range(j, 8):
                    a[j, m] = a[j, m] - (f0[i, j] * a[i, m] + f1[i, j] * a[k, m])
                e[j] = e[j] - (f0[i, j] * e[i] + f1[i, j] * e[k])
            w[i] = (s * e[i] - r * e[k]) * over
            w[k] = (p * e[k] - r * e[i]) * over
        if q < last:
            for i in (4, 2, 0):
                for j in range(i + 2, 8):
                    w[i] = w[i] - f0[i, j] * w[j]
                    w[i + 1] = w[i + 1] - f1[i, j] * w[j]
            for t in range(q + 1, last + 1):
                s = [col(tiles[t], c0 + j) * w[j] for j in range(8)]
                s = ((s[0] + s[1]) + (s[2] + s[3])) + ((s[4] + s[5]) + (s[6] + s[7]))
                tiles[t] = jnp.where(block, 0.0, tiles[t]) - s
        for i in range(0, 8, 2):
            k = i + 1
            p, r, s = a[i, i], a[i, k], a[k, k]
            ratio = r / p
            first = e[i] * lax.rsqrt(p)
            second = (e[k] - ratio * e[i]) * lax.rsqrt(s - ratio * r)
            out[c0 + i : c0 + i + 1, :] = jnp.where(lane <= c0 + i, first, 0.0)[0:1]
            out[c0 + k : c0 + k + 1, :] = jnp.where(lane <= c0 + k, second, 0.0)[0:1]


def factor_kernel(gall, slab, x, piv, w, inv, r):
    blocks = K // B
    at = lambda i: slice(i * B, i * B + B)
    band = lambda chip, d: gall[chip % CHIPS, :, at(d)]
    for i in range(blocks):
        for j in range(i, blocks):
            d = j - i
            if d <= 2:
                g = band(i, d)
            elif d == 3:
                g = band(i + 1, 3)
            elif d == 4:
                g = band(i + 2, 4)
            elif d == 5:
                g = band(j + 1, 3).T
            else:
                g = band(j, 8 - d).T
            w[at(i), at(j)] = g
    w[:, K:] = slab[...]
    eye = lax.broadcasted_iota(jnp.int32, (B, B), 0) == lax.broadcasted_iota(jnp.int32, (B, B), 1)
    scale = math.sqrt(ROWS)

    @pl.loop(0, blocks)
    def _(k):
        r0 = pl.multiple_of(k * B, B)
        eliminate(w[pl.ds(r0, B), pl.ds(r0, B)], inv)
        li = inv[...]
        diagonal = jnp.sum(jnp.where(eye, li, 0.0), axis=0, keepdims=True)
        piv[pl.ds(k, 1), :] = -jnp.log(diagonal) - 0.5 * math.log(ROWS)
        for kk in range(blocks):

            @pl.when(k == kk)
            def _():
                lo = kk * B
                r[:, lo + B :] = dot(li, w[lo : lo + B, lo + B :], 1, 0)
                for i in range(kk + 1, blocks):
                    w[at(i), i * B :] -= dot(r[:, at(i)], r[:, i * B :], 0, 0)
                x[at(kk), :] = r[:, K:] * scale


def hand_kernel(cuts, x, start, piv, handed, exponents, running, allp, xs, xr, vs, vr):
    me = lax.axis_index("col")
    c = lax.axis_index("cuts")
    barrier = pltpu.get_barrier_semaphore()
    for o in range(1, cuts):
        pl.semaphore_signal(
            barrier, inc=1, device_id={"cuts": lax.rem(c + o, cuts), "col": me}, device_id_type=MESH
        )

    @pl.when(c > 0)
    def _():
        for i in range(COL):
            pl.semaphore_signal(barrier, inc=1, device_id={"cuts": c - 1, "col": i}, device_id_type=MESH)

    pl.semaphore_wait(barrier, jnp.where(c < cuts - 1, cuts - 1 + COL, cuts - 1))

    my_cols = pl.ds(pl.multiple_of(me * B, B), B)
    give = []
    for o in range(1, cuts):
        s = remote(piv, allp.at[c], vs.at[o], vr.at[o], {"cuts": lax.rem(c + o, cuts), "col": me})
        s.start()
        give.append(s)
    allp[c] = piv[...]

    @pl.when(c < cuts - 1)
    def _():
        for o in range(COL):
            i = lax.rem(me + o, COL)
            remote(
                x.at[pl.ds(pl.multiple_of(i * HALF, HALF), HALF)], handed.at[:, my_cols],
                xs.at[o], xr.at[o], {"cuts": c + 1, "col": i},
            ).start()

    @pl.when(c == 0)
    def _():
        handed[...] = start[...]

    for o in range(1, cuts):
        come = allp.at[lax.rem(c + cuts - o, cuts)]
        remote(come, come, vs.at[o], vr.at[o], {"cuts": lax.rem(c + o, cuts), "col": me}).wait_recv()
    total = allp[0]
    for o in range(1, cuts):
        total = total + allp[o]
    expo = total / (SLICES * cuts)
    lane = lax.broadcasted_iota(jnp.int32, (B, B), 1)
    upto = jnp.where(lax.broadcasted_iota(jnp.int32, (B, B), 0) <= lane, 1.0, 0.0).astype(f32)
    sums = dot(expo, upto, 1, 0)
    before = jnp.zeros((1, 1), f32)
    parts = []
    for i in range(K // B):
        parts.append(sums[i : i + 1, :] + before)
        before = before + sums[i : i + 1, B - 1 : B]
    cumulated = jnp.concatenate(parts, axis=0)
    place = lax.broadcasted_iota(jnp.int32, (K // B, B), 0) * B + lax.broadcasted_iota(jnp.int32, (K // B, B), 1)
    means = cumulated / (place + 1).astype(f32)
    here = lax.broadcasted_iota(jnp.int32, (K // B, B), 0) == me // 2
    for value, out in ((expo, exponents), (means, running)):
        line = jnp.sum(jnp.where(here, value, 0.0), axis=0, keepdims=True)
        out[...] = jnp.where(me % 2 == 0, line[:, :HALF], line[:, HALF:])

    @pl.when(c > 0)
    def _():
        for o in range(COL):
            j = lax.rem(me + COL - o, COL)
            come = handed.at[:, pl.ds(pl.multiple_of(j * B, B), B)]
            remote(come, come, xs.at[o], xr.at[o], {"cuts": c - 1, "col": j}).wait_recv()

    @pl.when(c < cuts - 1)
    def _():
        for o in range(COL):
            i = lax.rem(me + o, COL)
            rows = x.at[pl.ds(pl.multiple_of(i * HALF, HALF), HALF)]
            remote(rows, handed.at[:, my_cols], xs.at[o], xr.at[o], {"cuts": c + 1, "col": i}).wait_send()

    for s in give:
        s.wait_send()


def local(cuts, levels, start_basis):
    start = start_basis[0]
    dma = pltpu.SemaphoreType.DMA
    slab, gall = pl.pallas_call(
        gram_kernel,
        out_shape=(jax.ShapeDtypeStruct((K, B), f32), jax.ShapeDtypeStruct((CHIPS, B, BANDS), f32)),
        in_specs=[VMEM] * 2,
        out_specs=(VMEM,) * 2,
        scratch_shapes=[
            pltpu.VMEM((HALF, ROWS), f32),
            pltpu.VMEM((5, B, SITES), f32),
            pltpu.VMEM((B, BANDS), f32),
            pltpu.VMEM((HALF, BANDS), f32),
            dma((5,)), dma((10,)), dma((4,)), dma((COL,)), dma((COL,)),
            dma, dma, dma((9,)), dma((9,)), dma((9,)), dma((9,)),
        ],
        compiler_params=pltpu.CompilerParams(
            collective_id=1, has_side_effects=True, vmem_limit_bytes=32 << 20
        ),
        name="gram",
    )(levels, start)
    x, piv = pl.pallas_call(
        factor_kernel,
        out_shape=(jax.ShapeDtypeStruct((K, B), f32), jax.ShapeDtypeStruct((K // B, B), f32)),
        in_specs=[VMEM] * 2,
        out_specs=(VMEM,) * 2,
        scratch_shapes=[pltpu.VMEM((K, K + B), f32), pltpu.VMEM((B, B), f32), pltpu.VMEM((B, K + B), f32)],
        compiler_params=pltpu.CompilerParams(vmem_limit_bytes=32 << 20),
        name="factor",
    )(gall, slab)
    handed, exponents, running = pl.pallas_call(
        functools.partial(hand_kernel, cuts),
        out_shape=(
            jax.ShapeDtypeStruct((HALF, ROWS), f32),
            jax.ShapeDtypeStruct((1, HALF), f32),
            jax.ShapeDtypeStruct((1, HALF), f32),
        ),
        in_specs=[VMEM] * 3,
        out_specs=(VMEM,) * 3,
        scratch_shapes=[
            pltpu.VMEM((cuts, K // B, B), f32),
            dma((COL,)), dma((COL,)), dma((cuts,)), dma((cuts,)),
        ],
        compiler_params=pltpu.CompilerParams(
            collective_id=2, has_side_effects=True, vmem_limit_bytes=32 << 20
        ),
        name="hand",
    )(x, start, piv)
    return exponents[0], running[0], handed[None]


def solution(mesh):
    in_specs = (P("cuts", None), P("cuts", "col", None))
    out_specs = (P("col"), P("col"), P("cuts", "col", None))
    return jax.shard_map(
        functools.partial(local, mesh.shape["cuts"]), mesh=mesh, in_specs=in_specs, out_specs=out_specs, check_vma=False
    )
```

time: 594 us -> 153 us (0.26)
  the two profiles are of different devices: /device:TPU:8 before, /device:TPU:5 now
where the time goes in v1:
time: 153 us; the launch traced here: 152 us
  Pallas kernels  148 us (97%)
  local copies, waits for them, and re-layouts  3.55 us (2%)
    pallas_call x1, Pallas kernels, local(): pl.pallas_call(gram_kernel, out_shape=(jax.ShapeDtypeStruct((K, B), f32),...  67.8 us
    pallas_call x1, Pallas kernels, local(): pl.pallas_call(factor_kernel, out_shape=(jax.ShapeDtypeStruct((K, B), f32...  44.6 us
    pallas_call x1, Pallas kernels, local(): pl.pallas_call(functools.partial(hand_kernel, cuts), out_shape=(jax.Shape...  35.8 us
    unnamed x9, local copies, waits for them, and re-layouts  3.55 us

profile of v1, /device:TPU:5, one launch (start us, length us, event | category | flops | bytes accessed | tf_op | source)
XLA Modules:
  0.0 152.4 jit_solution(16984611330872989156)
XLA Ops:
  0.6 0.0 copy-start
  0.6 1.0 copy-done
  1.7 0.0 copy-start.2
  1.7 0.7 copy-done.2
  2.4 0.0 copy-start.1
  2.4 67.8 %gram.1 = (f32[1024,128]{1,0:T(8,128)S(1)}, f32[8,128,640]{2,1,0:T(8,128)S(1)}) custom-call(s32[2,1024]{1,0:T(2,128)S(1)} %copy-done.2, f32[64,2048]{1,0:T(8,128)S(1)} %bitcast.4), custom_call_target="tpu_custom_call" | custom-call | tf_op jit(solution)/shard_map/gram/pallas_call | solution.py:340
  70.2 44.6 %factor.1 = (f32[1024,128]{1,0:T(8,128)S(1)}, f32[8,128]{1,0:T(8,128)S(1)}) custom-call(f32[8,128,640]{2,1,0:T(8,128)S(1)} %get-tuple-element.10.gall, f32[1024,128]{1,0:T(8,128)S(1)} %get-tuple-element.11.slab), custom_call_target="tpu_custom_call" | custom-call | tf_op jit(solution)/shard_map/factor/pallas_call | solution.py:358
  114.8 0.0 copy-done.1
  114.8 35.8 %hand.1 = (f32[64,2048]{1,0:T(8,128)S(1)}, f32[1,64]{1,0:T(1,128)S(1)}, f32[1,64]{1,0:T(1,128)S(1)}) custom-call(f32[1024,128]{1,0:T(8,128)S(1)} %get-tuple-element.12.x, f32[64,2048]{1,0:T(8,128)S(1)} %bitcast.5, f32[8,128]{1,0:T(8,128)S(1)} %get-tuple-element.13.piv), custom_call_target="tpu_custom_call" | custom-call | tf_op jit(solution)/shard_map/hand/pallas_call | solution.py:367
  150.6 0.5 copy.8
  151.1 0.5 copy.9
  151.6 0.8 copy.10
Async XLA Ops:
  0.6 1.0 copy-start
  1.7 0.7 copy-start.2
  2.4 112.4 %copy-start.1 = (f32[1,64,2048]{2,1,0:T(8,128)S(1)}, f32[1,64,2048]{2,1,0:T(8,128)}, u32[]{:S(2)}) copy-start(f32[1,64,2048]{2,1,0:T(8,128)} %param.3) | copy-start | bytes 1572868

commit v2 on v1

--- a/solution.py
+++ b/solution.py
@@ -26,6 +26,7 @@
 MESH = pl.DeviceIdType.MESH
 VMEM = pl.BlockSpec(memory_space=pltpu.VMEM)
 f32 = jnp.float32
+bf16 = jnp.bfloat16
 
 
 def dot(a, b, ca, cb):
@@ -112,14 +113,20 @@
     slab[my_rows, :] = prop[:, pl.ds(pl.multiple_of(me * B, B), B)]
 
     remote(gat.at[0, theirs], gat.at[0, theirs], gs.at[0], gr.at[1 - h], {"col": partner}).wait_recv()
+    def lower(d, first, second):
+        a = z if d < 3 else lax.rem(z + CHIPS + 2 - d, CHIPS)
+        wraps = a + d >= CHIPS
+        left = gat[jnp.where(wraps, first, second)]
+        part[:, d * B : d * B + B] = dot(left, gat[jnp.where(wraps, second, first)], 1, 1)
+
     part[:, 0:B] = dot(gat[0], gat[0], 1, 1)
-    part[:, B : 2 * B] = dot(gat[0], gat[3], 1, 1)
+    lower(1, 0, 3)
     for s in range(2):
         arrived(2, s)
         arrived(4, s)
-    part[:, 2 * B : 3 * B] = dot(gat[0], gat[4], 1, 1)
-    part[:, 3 * B : 4 * B] = dot(gat[1], gat[4], 1, 1)
-    part[:, 4 * B : 5 * B] = dot(gat[2], gat[4], 1, 1)
+    lower(2, 0, 4)
+    lower(3, 1, 4)
+    lower(4, 2, 4)
 
     both = remote(part.at[theirs], other, ps, pr, {"col": partner})
     both.start()
@@ -170,136 +177,135 @@
         s.wait_send()
 
 
-def eliminate(d, out):
+def tree(terms):
+    while len(terms) > 1:
+        pairs = [terms[i] + terms[i + 1] for i in range(0, len(terms) - 1, 2)]
+        terms = pairs + terms[len(pairs) * 2 :]
+    return terms[0]
+
+
+def eliminate(d, out, one):
     tiles = [d[8 * t : 8 * t + 8, :] for t in range(B // 8)]
     last = len(tiles) - 1
     lane = lax.broadcasted_iota(jnp.int32, (8, B), 1)
+    sub = lax.broadcasted_iota(jnp.int32, (8, B), 0)
     row = lambda v, i: jnp.broadcast_to(v[i : i + 1, :], (8, B))
     col = lambda v, c: jnp.broadcast_to(v[:, c : c + 1], (8, B))
-    for q, tile in enumerate(tiles):
-        tile = tiles[q]
+    at = [sub == i for i in range(8)]
+    pair = [jnp.logical_or(at[i], at[i + 1]) for i in range(0, 8, 2)]
+    odd = sub % 2 == 1
+    for q in range(last + 1):
         c0 = 8 * q
-        rows = [row(tile, j) for j in range(8)]
-        a = {(m, j): col(rows[m], c0 + j) for m in range(8) for j in range(m, 8)}
         block = jnp.logical_and(lane >= c0, lane < c0 + 8)
-        e = [jnp.where(block, jnp.where(lane == c0 + j, 1.0, 0.0), rows[j]) for j in range(8)]
-        f0, f1, w = {}, {}, [None] * 8
-        for i in range(0, 8, 2):
-            k = i + 1
-            p, r, s = a[i, i], a[i, k], a[k, k]
-            over = 1.0 / (p * s - r * r)
-            for j in range(k + 1, 8):
-                x, y = a[i, j], a[k, j]
-                f0[i, j] = (s * x - r * y) * over
-                f1[i, j] = (p * y - r * x) * over
-                for m in range(j, 8):
-                    a[j, m] = a[j, m] - (f0[i, j] * a[i, m] + f1[i, j] * a[k, m])
-                e[j] = e[j] - (f0[i, j] * e[i] + f1[i, j] * e[k])
-            w[i] = (s * e[i] - r * e[k]) * over
-            w[k] = (p * e[k] - r * e[i]) * over
+        v = [col(tiles[q], c0 + j) * one for j in range(8)]
+        strip = jnp.where(block, jnp.where(lane - c0 == sub, 1.0, 0.0), tiles[q])
+        rows = [row(strip, j) for j in range(8)]
+        u = [None] * 8
+        for p in range(4):
+            i, k = 2 * p, 2 * p + 1
+            a, r, e = row(v[i], i), row(v[i], k), row(v[k], k)
+            over = 1.0 / (a * e - r * r)
+            for j in range(i):
+                u[j] = v[j] if u[j] is None else jnp.where(pair[p], v[j], u[j])
+            if p == 0:
+                pa, pr, pe = a, r, e
+            else:
+                pa, pr, pe = (jnp.where(pair[p], x, y) for x, y in ((a, pa), (r, pr), (e, pe)))
+            if q == last and p == 3:
+                break
+            n0 = jnp.where(at[i], -e, jnp.where(at[k], r, e * v[i] - r * v[k])) * over
+            n1 = jnp.where(at[k], -a, jnp.where(at[i], r, a * v[k] - r * v[i])) * over
+            for j in range(8):
+                if j not in (i, k):
+                    v[j] = jnp.where(pair[p], 0.0, v[j]) - (n0 * row(v[j], i) + n1 * row(v[j], k))
+            v[i], v[k] = -n0, -n1
         if q < last:
-            for i in (4, 2, 0):
-                for j in range(i + 2, 8):
-                    w[i] = w[i] - f0[i, j] * w[j]
-                    w[i + 1] = w[i + 1] - f1[i, j] * w[j]
+            w = tree([v[j] * rows[j] for j in range(8)])
+            w = [row(w, j) for j in range(8)]
             for t in range(q + 1, last + 1):
-                s = [col(tiles[t], c0 + j) * w[j] for j in range(8)]
-                s = ((s[0] + s[1]) + (s[2] + s[3])) + ((s[4] + s[5]) + (s[6] + s[7]))
-                tiles[t] = jnp.where(block, 0.0, tiles[t]) - s
-        for i in range(0, 8, 2):
-            k = i + 1
-            p, r, s = a[i, i], a[i, k], a[k, k]
-            ratio = r / p
-            first = e[i] * lax.rsqrt(p)
-            second = (e[k] - ratio * e[i]) * lax.rsqrt(s - ratio * r)
-            out[c0 + i : c0 + i + 1, :] = jnp.where(lane <= c0 + i, first, 0.0)[0:1]
-            out[c0 + k : c0 + k + 1, :] = jnp.where(lane <= c0 + k, second, 0.0)[0:1]
-
-
-def factor_kernel(gall, slab, x, piv, w, inv, r):
+                taken = tree([col(tiles[t], c0 + j) * w[j] for j in range(8)])
+                tiles[t] = jnp.where(block, 0.0, tiles[t]) - taken
+        forward = strip + tree([jnp.where(sub >= j + 2 - j % 2, u[j], 0.0) * rows[j] for j in range(6)])
+        ratio = pr / pa
+        second = (forward - ratio * pltpu.roll(forward, 1, 0)) * lax.rsqrt(pe - ratio * pr)
+        scaled = jnp.where(odd, second, forward * lax.rsqrt(pa))
+        out[c0 : c0 + 8, :] = jnp.where(lane <= c0 + sub, scaled, 0.0)
+
+
+def split(x):
+    a = x.astype(bf16)
+    rest = x - a.astype(f32)
+    b = rest.astype(bf16)
+    return a, b, (rest - b.astype(f32)).astype(bf16)
+
+
+def product(x, y, transposed=True):
+    c = 1 if transposed else 0
+    one = lambda a, b: lax.dot_general(a, b, (((1,), (c,)), ((), ())), preferred_element_type=f32)
+    two = jnp.concatenate([y[0], y[1]], axis=1 - c)
+    n = two.shape[1 - c] // 2
+    high, mid = one(x[0], two), one(x[1], two)
+    return ((one(x[0], y[2]) + one(x[2], y[0])) + mid[:, n:]) + (mid[:, :n] + high[:, n:]) + high[:, :n]
+
+
+def at(i):
+    return slice(i * B, i * B + B)
+
+
+def factor_steps(g, slab, x, piv, ls, xs, cs, inv, ones, ready, given):
+    eye = lax.broadcasted_iota(jnp.int32, (B, B), 0) == lax.broadcasted_iota(jnp.int32, (B, B), 1)
     blocks = K // B
-    at = lambda i: slice(i * B, i * B + B)
-    band = lambda chip, d: gall[chip % CHIPS, :, at(d)]
-    for i in range(blocks):
-        for j in range(i, blocks):
-            d = j - i
-            if d <= 2:
-                g = band(i, d)
-            elif d == 3:
-                g = band(i + 1, 3)
-            elif d == 4:
-                g = band(i + 2, 4)
-            elif d == 5:
-                g = band(j + 1, 3).T
-            else:
-                g = band(j, 8 - d).T
-            w[at(i), at(j)] = g
-    w[:, K:] = slab[...]
-    eye = lax.broadcasted_iota(jnp.int32, (B, B), 0) == lax.broadcasted_iota(jnp.int32, (B, B), 1)
-    scale = math.sqrt(ROWS)
-
-    @pl.loop(0, blocks)
-    def _(k):
-        r0 = pl.multiple_of(k * B, B)
-        eliminate(w[pl.ds(r0, B), pl.ds(r0, B)], inv)
-        li = inv[...]
-        diagonal = jnp.sum(jnp.where(eye, li, 0.0), axis=0, keepdims=True)
-        piv[pl.ds(k, 1), :] = -jnp.log(diagonal) - 0.5 * math.log(ROWS)
-        for kk in range(blocks):
-
-            @pl.when(k == kk)
-            def _():
-                lo = kk * B
-                r[:, lo + B :] = dot(li, w[lo : lo + B, lo + B :], 1, 0)
-                for i in range(kk + 1, blocks):
-                    w[at(i), i * B :] -= dot(r[:, at(i)], r[:, i * B :], 0, 0)
-                x[at(kk), :] = r[:, K:] * scale
-
-
-def hand_kernel(cuts, x, start, piv, handed, exponents, running, allp, xs, xr, vs, vr):
-    me = lax.axis_index("col")
-    c = lax.axis_index("cuts")
-    barrier = pltpu.get_barrier_semaphore()
-    for o in range(1, cuts):
-        pl.semaphore_signal(
-            barrier, inc=1, device_id={"cuts": lax.rem(c + o, cuts), "col": me}, device_id_type=MESH
-        )
-
-    @pl.when(c > 0)
-    def _():
-        for i in range(COL):
-            pl.semaphore_signal(barrier, inc=1, device_id={"cuts": c - 1, "col": i}, device_id_type=MESH)
-
-    pl.semaphore_wait(barrier, jnp.where(c < cuts - 1, cuts - 1 + COL, cuts - 1))
-
-    my_cols = pl.ds(pl.multiple_of(me * B, B), B)
-    give = []
-    for o in range(1, cuts):
-        s = remote(piv, allp.at[c], vs.at[o], vr.at[o], {"cuts": lax.rem(c + o, cuts), "col": me})
-        s.start()
-        give.append(s)
-    allp[c] = piv[...]
-
-    @pl.when(c < cuts - 1)
-    def _():
-        for o in range(COL):
-            i = lax.rem(me + o, COL)
-            remote(
-                x.at[pl.ds(pl.multiple_of(i * HALF, HALF), HALF)], handed.at[:, my_cols],
-                xs.at[o], xr.at[o], {"cuts": c + 1, "col": i},
-            ).start()
-
-    @pl.when(c == 0)
-    def _():
-        handed[...] = start[...]
-
-    for o in range(1, cuts):
-        come = allp.at[lax.rem(c + cuts - o, cuts)]
-        remote(come, come, vs.at[o], vr.at[o], {"cuts": lax.rem(c + o, cuts), "col": me}).wait_recv()
-    total = allp[0]
-    for o in range(1, cuts):
-        total = total + allp[o]
-    expo = total / (SLICES * cuts)
+    three = range(3)
+    ones[...] = jnp.ones_like(ones)
+    one = ones[...]
+    for k in range(blocks):
+        rest, done = slice((k + 1) * B, K), slice(0, k * B)
+        ready(k)
+        if k == 0:
+            d = g[at(0), at(0)]
+        else:
+            column = split(product(split(cs[k * B : K, :]), li))
+            for s in three:
+                ls[s, k * B : K, at(k - 1)] = column[s]
+            lk = [ls[s, at(k), done] for s in three]
+        xp = slab[at(k), :]
+        if k:
+            xp = xp - product(lk, [xs[s, done, :] for s in three], False)
+        if k < blocks - 1:
+            c = g[rest, at(k)]
+            later = g[at(k + 1), at(k + 1)]
+            if k:
+                c = c - product([ls[s, rest, done] for s in three], lk)
+                ln = [ls[s, at(k + 1), done] for s in three]
+                later = later - product(ln, ln)
+            cs[rest, :] = c
+        eliminate(d, inv, one)
+        inverse = inv[...]
+        li = split(inverse)
+        if k < blocks - 1:
+            l1 = split(product(split(cs[at(k + 1), :]), li))
+            d = later - product(l1, l1)
+        solved = product(li, split(xp), False)
+        x[at(k), :] = solved * math.sqrt(ROWS)
+        if k < blocks - 1:
+            solved = split(solved)
+            for s in three:
+                xs[s, at(k), :] = solved[s]
+        diagonal = jnp.sum(jnp.where(eye, inverse, 0.0), axis=0, keepdims=True)
+        piv[k : k + 1, :] = -jnp.log(diagonal) - 0.5 * math.log(ROWS)
+        given(k)
+
+
+def place_bands(gall, g):
+    for i in range(K // B):
+        for j in range(i + 1):
+            d = i - j
+            chip = (j, j, j, j + 1, j + 2, i + 1, i, i)[d]
+            band = d if d <= 4 else 8 - d
+            g[at(i), at(j)] = gall[chip % CHIPS, :, at(band)]
+
+
+def means_of(expo):
     lane = lax.broadcasted_iota(jnp.int32, (B, B), 1)
     upto = jnp.where(lax.broadcasted_iota(jnp.int32, (B, B), 0) <= lane, 1.0, 0.0).astype(f32)
     sums = dot(expo, upto, 1, 0)
@@ -308,9 +314,70 @@
     for i in range(K // B):
         parts.append(sums[i : i + 1, :] + before)
         before = before + sums[i : i + 1, B - 1 : B]
-    cumulated = jnp.concatenate(parts, axis=0)
     place = lax.broadcasted_iota(jnp.int32, (K // B, B), 0) * B + lax.broadcasted_iota(jnp.int32, (K // B, B), 1)
-    means = cumulated / (place + 1).astype(f32)
+    return jnp.concatenate(parts, axis=0) / (place + 1).astype(f32)
+
+
+def factor_kernel(
+    cuts, gall, slab, start, handed, exponents, running,
+    g, x, piv, allp, ls, xs, cs, inv, ones, xss, xrs, vs, vr,
+):
+    me = lax.axis_index("col")
+    c = lax.axis_index("cuts")
+    barrier = pltpu.get_barrier_semaphore()
+    for o in range(1, cuts):
+        pl.semaphore_signal(
+            barrier, inc=1, device_id={"cuts": lax.rem(c + o, cuts), "col": me}, device_id_type=MESH
+        )
+
+    @pl.when(c > 0)
+    def _():
+        for i in range(COL):
+            pl.semaphore_signal(barrier, inc=1, device_id={"cuts": c - 1, "col": i}, device_id_type=MESH)
+
+    place_bands(gall, g)
+
+    @pl.when(c == 0)
+    def _():
+        handed[...] = start[...]
+
+    my_cols = pl.ds(pl.multiple_of(me * B, B), B)
+
+    def rows_out(i):
+        return remote(
+            x.at[pl.ds(i * HALF, HALF)], handed.at[:, my_cols], xss.at[i], xrs.at[me], {"cuts": c + 1, "col": i}
+        )
+
+    def ready(k):
+        if k == 1:
+            pl.semaphore_wait(barrier, jnp.where(c < cuts - 1, cuts - 1 + COL, cuts - 1))
+
+            @pl.when(c < cuts - 1)
+            def _():
+                rows_out(0).start()
+                rows_out(1).start()
+
+    def given(k):
+        if k:
+
+            @pl.when(c < cuts - 1)
+            def _():
+                rows_out(2 * k).start()
+                rows_out(2 * k + 1).start()
+
+    factor_steps(g, slab, x, piv, ls, xs, cs, inv, ones, ready, given)
+
+    give = []
+    for o in range(1, cuts):
+        s = remote(piv, allp.at[c], vs.at[o], vr.at[o], {"cuts": lax.rem(c + o, cuts), "col": me})
+        s.start()
+        give.append(s)
+    allp[c] = piv[...]
+    for o in range(1, cuts):
+        come = allp.at[lax.rem(c + cuts - o, cuts)]
+        remote(come, come, vs.at[o], vr.at[o], {"cuts": lax.rem(c + o, cuts), "col": me}).wait_recv()
+    expo = tree([allp[o] for o in range(cuts)]) / (SLICES * cuts)
+    means = means_of(expo)
     here = lax.broadcasted_iota(jnp.int32, (K // B, B), 0) == me // 2
     for value, out in ((expo, exponents), (means, running)):
         line = jnp.sum(jnp.where(here, value, 0.0), axis=0, keepdims=True)
@@ -318,17 +385,14 @@
 
     @pl.when(c > 0)
     def _():
-        for o in range(COL):
-            j = lax.rem(me + COL - o, COL)
-            come = handed.at[:, pl.ds(pl.multiple_of(j * B, B), B)]
-            remote(come, come, xs.at[o], xr.at[o], {"cuts": c - 1, "col": j}).wait_recv()
+        for j in range(COL):
+            come = handed.at[:, pl.ds(j * B, B)]
+            remote(come, come, xss.at[j], xrs.at[j], {"cuts": c - 1, "col": j}).wait_recv()
 
     @pl.when(c < cuts - 1)
     def _():
-        for o in range(COL):
-            i = lax.rem(me + o, COL)
-            rows = x.at[pl.ds(pl.multiple_of(i * HALF, HALF), HALF)]
-            remote(rows, handed.at[:, my_cols], xs.at[o], xr.at[o], {"cuts": c + 1, "col": i}).wait_send()
+        for i in range(COL):
+            rows_out(i).wait_send()
 
     for s in give:
         s.wait_send()
@@ -355,17 +419,8 @@
         ),
         name="gram",
     )(levels, start)
-    x, piv = pl.pallas_call(
-        factor_kernel,
-        out_shape=(jax.ShapeDtypeStruct((K, B), f32), jax.ShapeDtypeStruct((K // B, B), f32)),
-        in_specs=[VMEM] * 2,
-        out_specs=(VMEM,) * 2,
-        scratch_shapes=[pltpu.VMEM((K, K + B), f32), pltpu.VMEM((B, B), f32), pltpu.VMEM((B, K + B), f32)],
-        compiler_params=pltpu.CompilerParams(vmem_limit_bytes=32 << 20),
-        name="factor",
-    )(gall, slab)
     handed, exponents, running = pl.pallas_call(
-        functools.partial(hand_kernel, cuts),
+        functools.partial(factor_kernel, cuts),
         out_shape=(
             jax.ShapeDtypeStruct((HALF, ROWS), f32),
             jax.ShapeDtypeStruct((1, HALF), f32),
@@ -374,14 +429,22 @@
         in_specs=[VMEM] * 3,
         out_specs=(VMEM,) * 3,
         scratch_shapes=[
+            pltpu.VMEM((K, K), f32),
+            pltpu.VMEM((K, B), f32),
+            pltpu.VMEM((K // B, B), f32),
             pltpu.VMEM((cuts, K // B, B), f32),
+            pltpu.VMEM((3, K, K), bf16),
+            pltpu.VMEM((3, K, B), bf16),
+            pltpu.VMEM((K, B), f32),
+            pltpu.VMEM((B, B), f32),
+            pltpu.VMEM((8, B), f32),
             dma((COL,)), dma((COL,)), dma((cuts,)), dma((cuts,)),
         ],
         compiler_params=pltpu.CompilerParams(
-            collective_id=2, has_side_effects=True, vmem_limit_bytes=32 << 20
+            collective_id=2, has_side_effects=True, vmem_limit_bytes=40 << 20
         ),
-        name="hand",
-    )(x, start, piv)
+        name="factor",
+    )(gall, slab, start)
     return exponents[0], running[0], handed[None]
 
 

time: 153 us -> 120 us (0.78)
  the two profiles are of different devices: /device:TPU:5 before, /device:TPU:1 now
where the time goes in v2:
time: 120 us
  Pallas kernels  115 us (96%)
  local copies, waits for them, and re-layouts  4.59 us (4%)
    pallas_call x1, Pallas kernels, local(): pl.pallas_call(gram_kernel, out_shape=(jax.ShapeDtypeStruct((K, B), f32),...  68.5 us
    pallas_call x1, Pallas kernels, local(): pl.pallas_call(functools.partial(factor_kernel, cuts), out_shape=(jax.Sha...  46.1 us
    unnamed x9, local copies, waits for them, and re-layouts  4.59 us

profile of v2, /device:TPU:1, one launch (start us, length us, event | category | flops | bytes accessed | tf_op | source)
XLA Modules:
  0.0 119.9 jit_solution(12465462745118721984)
XLA Ops:
  0.6 0.0 copy-start
  0.6 1.0 copy-done
  1.7 0.0 copy-start.2
  1.7 0.7 copy-done.2
  2.4 68.5 %gram.1 = (f32[1024,128]{1,0:T(8,128)S(1)}, f32[8,128,640]{2,1,0:T(8,128)S(1)}) custom-call(s32[2,1024]{1,0:T(2,128)S(1)} %copy-done.2, f32[64,2048]{1,0:T(8,128)S(1)} %bitcast.4), custom_call_target="tpu_custom_call" | custom-call | tf_op jit(solution)/shard_map/gram/pallas_call | solution.py:404
  70.9 0.0 copy-start.1
  70.9 1.0 copy-done.1
  72.0 46.1 %factor.1 = (f32[64,2048]{1,0:T(8,128)S(1)}, f32[1,64]{1,0:T(1,128)S(1)}, f32[1,64]{1,0:T(1,128)S(1)}) custom-call(f32[8,128,640]{2,1,0:T(8,128)S(1)} %get-tuple-element.8.gall, f32[1024,128]{1,0:T(8,128)S(1)} %get-tuple-element.9.slab, f32[64,2048]{1,0:T(8,128)S(1)} %bitcast.5), custom_call_target="tpu_custom_call" | custom-call | tf_op jit(solution)/shard_map/factor/pallas_call | solution.py:422
  118.1 0.5 copy.8
  118.6 0.5 copy.9
  119.1 0.8 copy.10
Async XLA Ops:
  0.6 1.0 copy-start
  1.7 0.7 copy-start.2
  70.9 1.0 copy-start.1

commit v3 on v2

v3 whole, which is shorter than its diff:
```python
import functools
import math

import jax
import jax.numpy as jnp
from jax import lax
from jax.experimental import pallas as pl
from jax.experimental.pallas import tpu as pltpu
from jax.sharding import PartitionSpec as P

M = 32
SITES = 1024
ROWS = 2048
SLICES = 2
B = 128
HALF = 64
CHIPS = 8
COL = 16
K = 1024
BANDS = 6 * B
LAG = 4
WAIT = 2

energy = 0.5
disorder = 4.0
level_span = 65536.0

MESH = pl.DeviceIdType.MESH
VMEM = pl.BlockSpec(memory_space=pltpu.VMEM)
f32 = jnp.float32
bf16 = jnp.bfloat16


def dot(a, b, ca, cb):
    return lax.dot_general(
        a, b, (((ca,), (cb,)), ((), ())), precision=lax.Precision.HIGHEST, preferred_element_type=f32
    )


def remote(src, dst, send, recv, device):
    return pltpu.make_async_remote_copy(
        src_ref=src, dst_ref=dst, send_sem=send, recv_sem=recv, device_id=device, device_id_type=MESH
    )


def neighbours(x):
    site = lax.broadcasted_iota(jnp.int32, x.shape, 1)
    b = lax.rem(site, M)
    around = lambda by: pltpu.roll(x, by % SITES, 1)
    along = jnp.where(b == 0, around(1 - M), around(1)) + jnp.where(b == M - 1, around(M - 1), around(-1))
    return along + around(M) + around(-M)


def tree(terms):
    while len(terms) > 1:
        pairs = [terms[i] + terms[i + 1] for i in range(0, len(terms) - 1, 2)]
        terms = pairs + terms[len(pairs) * 2 :]
    return terms[0]


def eliminate(d, out, one):
    tiles = [d[8 * t : 8 * t + 8, :] for t in range(B // 8)]
    last = len(tiles) - 1
    lane = lax.broadcasted_iota(jnp.int32, (8, B), 1)
    sub = lax.broadcasted_iota(jnp.int32, (8, B), 0)
    row = lambda v, i: jnp.broadcast_to(v[i : i + 1, :], (8, B))
    col = lambda v, c: jnp.broadcast_to(v[:, c : c + 1], (8, B))
    at = [sub == i for i in range(8)]
    pair = [jnp.logical_or(at[i], at[i + 1]) for i in range(0, 8, 2)]
    odd = sub % 2 == 1
    for q in range(last + 1):
        c0 = 8 * q
        block = jnp.logical_and(lane >= c0, lane < c0 + 8)
        v = [col(tiles[q], c0 + j) * one for j in range(8)]
        strip = jnp.where(block, jnp.where(lane - c0 == sub, 1.0, 0.0), tiles[q])
        rows = [row(strip, j) for j in range(8)]
        u = [None] * 8
        for p in range(4):
            i, k = 2 * p, 2 * p + 1
            a, r, e = row(v[i], i), row(v[i], k), row(v[k], k)
            over = 1.0 / (a * e - r * r)
            for j in range(i):
                u[j] = v[j] if u[j] is None else jnp.where(pair[p], v[j], u[j])
            if p == 0:
                pa, pr, pe = a, r, e
            else:
                pa, pr, pe = (jnp.where(pair[p], x, y) for x, y in ((a, pa), (r, pr), (e, pe)))
            if q == last and p == 3:
                break
            n0 = jnp.where(at[i], -e, jnp.where(at[k], r, e * v[i] - r * v[k])) * over
            n1 = jnp.where(at[k], -a, jnp.where(at[i], r, a * v[k] - r * v[i])) * over
            for j in range(8):
                if j not in (i, k):
                    v[j] = jnp.where(pair[p], 0.0, v[j]) - (n0 * row(v[j], i) + n1 * row(v[j], k))
            v[i], v[k] = -n0, -n1
        if q < last:
            w = tree([v[j] * rows[j] for j in range(8)])
            w = [row(w, j) for j in range(8)]
            for t in range(q + 1, last + 1):
                taken = tree([col(tiles[t], c0 + j) * w[j] for j in range(8)])
                tiles[t] = jnp.where(block, 0.0, tiles[t]) - taken
        forward = strip + tree([jnp.where(sub >= j + 2 - j % 2, u[j], 0.0) * rows[j] for j in range(6)])
        ratio = pr / pa
        second = (forward - ratio * pltpu.roll(forward, 1, 0)) * lax.rsqrt(pe - ratio * pr)
        scaled = jnp.where(odd, second, forward * lax.rsqrt(pa))
        out[c0 : c0 + 8, :] = jnp.where(lane <= c0 + sub, scaled, 0.0)


def split(x):
    a = x.astype(bf16)
    rest = x - a.astype(f32)
    b = rest.astype(bf16)
    return a, b, (rest - b.astype(f32)).astype(bf16)


def product(x, y, transposed=True):
    c = 1 if transposed else 0
    one = lambda a, b: lax.dot_general(a, b, (((1,), (c,)), ((), ())), preferred_element_type=f32)
    two = jnp.concatenate([y[0], y[1]], axis=1 - c)
    n = two.shape[1 - c] // 2
    high, mid = one(x[0], two), one(x[1], two)
    return ((one(x[0], y[2]) + one(x[2], y[0])) + mid[:, n:]) + (mid[:, :n] + high[:, n:]) + high[:, :n]


def at(i):
    return slice(i * B, i * B + B)


def means_of(expo):
    lane = lax.broadcasted_iota(jnp.int32, (B, B), 1)
    upto = jnp.where(lax.broadcasted_iota(jnp.int32, (B, B), 0) <= lane, 1.0, 0.0).astype(f32)
    sums = dot(expo, upto, 1, 0)
    before = jnp.zeros((1, 1), f32)
    parts = []
    for i in range(K // B):
        parts.append(sums[i : i + 1, :] + before)
        before = before + sums[i : i + 1, B - 1 : B]
    place = lax.broadcasted_iota(jnp.int32, (K // B, B), 0) * B + lax.broadcasted_iota(jnp.int32, (K // B, B), 1)
    return jnp.concatenate(parts, axis=0) / (place + 1).astype(f32)


def sweep_kernel(
    cuts, lev, start, handed, exponents, running,
    prop, gat, part, other, first, near, far, across, slab, x, piv, allp, ls, xs, cs, lis, inv, ones,
    gs, gr, fs, g2r, ps, pr, d0s, d0r, ns, nr, nis, nir, f3s, f3r, f3is, f3ir, f4s, f4r, f4is, f4ir,
    als, alr, xss, xrs, vs, vr,
):
    me = lax.axis_index("col")
    c = lax.axis_index("cuts")
    z, h = me // 2, me % 2
    up, down = lax.rem(z + 1, CHIPS), lax.rem(z + CHIPS - 1, CHIPS)
    partner = z * 2 + 1 - h
    mine = pl.ds(pl.multiple_of(h * HALF, HALF), HALF)
    theirs = pl.ds(pl.multiple_of((1 - h) * HALF, HALF), HALF)
    my_cols = pl.ds(pl.multiple_of(me * B, B), B)
    my_rows = pl.ds(pl.multiple_of(me * HALF, HALF), HALF)
    blocks = K // B
    sends = []

    barrier = pltpu.get_barrier_semaphore()
    for o in range(1, COL):
        pl.semaphore_signal(barrier, inc=1, device_id={"col": lax.rem(me + o, COL)}, device_id_type=MESH)
    for o in range(1, cuts):
        pl.semaphore_signal(
            barrier, inc=1, device_id={"cuts": lax.rem(c + o, cuts), "col": me}, device_id_type=MESH
        )

    @pl.when(c > 0)
    def _():
        for i in range(COL):
            pl.semaphore_signal(barrier, inc=1, device_id={"cuts": c - 1, "col": i}, device_id_type=MESH)

    upper = start[:, :SITES]
    lower = start[:, SITES:]
    for n in range(SLICES):
        onsite = disorder * (lev[n : n + 1, :].astype(f32) / level_span - 0.5)
        upper, lower = (energy - onsite) * upper - neighbours(upper) - lower, upper
    prop[:, :SITES] = upper
    prop[:, SITES:] = lower

    @pl.when(c == 0)
    def _():
        handed[...] = start[...]

    everyone = COL - 1 + cuts - 1
    pl.semaphore_wait(barrier, jnp.where(c < cuts - 1, everyone + COL, everyone))

    their_half = pl.ds(pl.multiple_of((1 - h) * SITES, SITES), SITES)
    swap = remote(prop.at[:, their_half], gat.at[0, mine], gs.at[4], gr.at[h], {"col": partner})
    swap.start()
    sends.append(swap)
    for way in range(2):
        for t, (slot, chip) in enumerate(((1, up), (3, down))):
            f = h if way == 0 else 1 - h
            half = prop.at[:, pl.ds(pl.multiple_of(f * SITES, SITES), SITES)]
            out = remote(half, gat.at[slot, mine], gs.at[2 * way + t], gr.at[2 * slot + h], {"col": chip * 2 + f})
            out.start()
            sends.append(out)
    gat[0, mine, :] = prop[:, pl.ds(pl.multiple_of(h * SITES, SITES), SITES)]

    def come(ref, sem):
        remote(ref, ref, gs.at[0], sem, {"col": partner}).wait_recv()

    def arrived(slot, s):
        come(gat.at[slot, pl.ds(pl.multiple_of(s * HALF, HALF), HALF)], gr.at[2 * slot + s])

    kinds = ((0, 0, 0, 0), (0, 1, 0, 3), (-1, 2, 1, 3), (-1, 3, 1, 4), (-2, 3, 2, 3), (-2, 4, 2, 4))

    def make(kind):
        offset, d, one, two = kinds[kind]
        if d == 0:
            value = dot(gat[one], gat[one], 1, 1)
        else:
            wraps = lax.rem(z + CHIPS + offset, CHIPS) + d >= CHIPS
            value = dot(gat[jnp.where(wraps, one, two)], gat[jnp.where(wraps, two, one)], 1, 1)
        part[:, kind * B : kind * B + B] = value

    def pair_sum(group, lo, hi):
        cols = pl.ds(lo * B, (hi - lo) * B)
        both = remote(part.at[theirs, cols], other.at[:, cols], ps.at[group], pr.at[group], {"col": partner})
        both.start()
        both.wait_recv()
        sends.append(both)
        return part[mine, lo * B : hi * B] + other[:, lo * B : hi * B]

    quarter = HALF // 2
    halves = [pl.ds(pl.multiple_of(h * HALF + q * quarter, quarter), quarter) for q in range(2)]
    their_halves = [pl.ds(pl.multiple_of((1 - h) * HALF + q * quarter, quarter), quarter) for q in range(2)]

    def near_step(d):
        rows = (mine, mine) if d < 4 else halves
        for way, (chip, to) in enumerate(
            ((lax.rem(z + CHIPS - d + 1, CHIPS), up), (lax.rem(z + d - 1, CHIPS), down))
        ):
            ref = near.at[chip, rows[way]]
            out = remote(ref, ref, ns.at[2 * d + way], nr.at[2 * d + way], {"col": to * 2 + h})
            out.start()
            sends.append(out)

    def near_inside(chip, rows, i):
        ref = near.at[chip, rows]
        out = remote(ref, ref, nis.at[i], nir.at[i], {"col": partner})
        out.start()
        sends.append(out)

    def near_chips(d):
        return lax.rem(z + CHIPS - d, CHIPS), lax.rem(z + d, CHIPS)

    def near_come(d):
        rows = (mine, mine) if d < 4 else halves
        for way, chip in enumerate(near_chips(d)):
            come(near.at[chip, rows[way]], nr.at[2 * d + way])
            near_inside(chip, rows[way], 2 * d + way)

    def far_place(way):
        return lax.rem(z + CHIPS - way, CHIPS)

    def far_out(way, o):
        ref = far.at[far_place(way), mine]
        to = lax.rem(z + (o if way else CHIPS - o), CHIPS)
        return remote(ref, ref, f3s.at[4 * way + o], f3r.at[4 * way + o], {"col": to * 2 + h})

    def far_from(way, o):
        return lax.rem(z + (CHIPS - o - 1 if way else o), CHIPS)

    def far_inside(way, o):
        ref = far.at[far_from(way, o), mine]
        return remote(ref, ref, f3is.at[4 * way + o], f3ir.at[4 * way + o], {"col": partner})

    steps4 = (1, CHIPS - 1, 2 + 4 * h)

    def across_of(chip):
        return lax.rem(chip + CHIPS - 2, CHIPS // 2)

    def across_out(i):
        ref = across.at[across_of(z), mine]
        return remote(ref, ref, f4s.at[i], f4r.at[i], {"col": lax.rem(z + steps4[i], CHIPS) * 2 + h})

    def across_from(i):
        return across_of(z) if i == 3 else across_of(lax.rem(z + CHIPS - steps4[i], CHIPS))

    def across_inside(i):
        ref = across.at[across_from(i), mine]
        return remote(ref, ref, f4is.at[i], f4ir.at[i], {"col": partner})

    def piece(n):
        s = h if n < 2 else 1 - h
        return pl.ds(pl.multiple_of(s * HALF + n % 2 * quarter, quarter), quarter)

    def second_hop(n):
        for way, (slot, chip) in enumerate(((1, up), (3, down))):
            out = remote(
                gat.at[slot, piece(n)], gat.at[slot + 1, piece(n)], fs.at[4 * way + n], g2r.at[4 * way + n],
                {"col": chip * 2 + h},
            )
            out.start()
            sends.append(out)

    def far_issue():
        for n in range(4):
            for way in range(2):
                come(gat.at[2 * way + 2, piece(n)], g2r.at[4 * way + n])
        make(3)
        make(4)
        make(5)
        late = pair_sum(2, 3, 6)
        far[far_place(0), mine, :] = late[:, :B]
        far[far_place(1), mine, :] = late[:, B : 2 * B]
        across[across_of(z), mine, :] = late[:, 2 * B :]
        for o in range(1, 4):
            far_out(0, o).start()
            far_out(1, o).start()
            if o < 3:
                across_out(o - 1).start()
        across_out(2).start()
        far_inside(0, 0).start()
        far_inside(1, 0).start()
        across_inside(3).start()

    def far_finish():
        for o in range(1, 4):
            for way in range(2):
                come(far.at[far_from(way, o), mine], f3r.at[4 * way + o])
                far_inside(way, o).start()
        for i in range(3):
            come(across.at[across_from(i), mine], f4r.at[i])
            across_inside(i).start()

    def far_complete():
        for o in range(4):
            for way in range(2):
                come(far.at[far_from(way, o), theirs], f3ir.at[4 * way + o])
        for i in range(4):
            n = across_of(z) if i == 3 else across_of(lax.rem(z + CHIPS - (1, CHIPS - 1, 6 - 4 * h)[i], CHIPS))
            come(across.at[n, theirs], f4ir.at[i])

    def columns_issue():
        for o in range(1, COL):
            out = columns_out(o)
            out.start()
            sends.append(out)
        slab[my_rows, :] = prop[:, my_cols]

    def gram_block(i, j):
        d = i - j
        if d <= 2 or d >= 6:
            chip, kind = (j, j, j + 1, 0, 0, 0, i + 1, i)[d], min(d, CHIPS - d)
            return near[chip % CHIPS, :, at(kind)]
        if d == 4:
            return across[j]
        return far[((j if d == 3 else i) + 1) % CHIPS]

    def columns_out(o):
        d = lax.rem(me + o, COL)
        cols = pl.ds(pl.multiple_of(d * B, B), B)
        return remote(prop.at[:, cols], slab.at[my_rows], als.at[o], alr.at[o], {"col": d})

    def rows_out(i):
        return remote(
            x.at[pl.ds(i * HALF, HALF)], handed.at[:, my_cols], xss.at[i], xrs.at[me], {"cuts": c + 1, "col": i}
        )

    come(gat.at[0, theirs], gr.at[1 - h])
    make(0)

    def first_out(o):
        ref = first.at[mine]
        return remote(ref, ref, d0s.at[o], d0r.at[h], {"col": lax.rem(me + o, COL)})

    diagonal_half = pair_sum(0, 0, 1)
    near[z, mine, 0:B] = diagonal_half

    @pl.when(z == 0)
    def _():
        first[mine, :] = diagonal_half
        for o in range(1, COL):
            first_out(o).start()

    arrived(1, h)
    arrived(3, h)
    second_hop(0)
    arrived(1, 1 - h)
    arrived(3, 1 - h)
    make(1)
    make(2)
    near[z, mine, B : 3 * B] = pair_sum(1, 1, 3)
    near_step(1)
    second_hop(1)
    near_inside(z, mine, 0)
    near_come(1)
    near_step(2)
    second_hop(2)

    @pl.when(z == 0)
    def _():
        come(first.at[theirs], d0r.at[1 - h])

    @pl.when(z > 0)
    def _():
        for s in range(2):
            come(first.at[pl.ds(s * HALF, HALF)], d0r.at[s])

    ones[...] = jnp.ones_like(ones)
    one = ones[...]
    eliminate(first[...], inv, one)

    near_come(2)
    near_step(3)
    second_hop(3)
    near_come(3)
    near_step(4)
    far_issue()
    columns_issue()
    near_come(4)
    for d in range(5):
        rows = (theirs, theirs) if d < 4 else their_halves
        for way, chip in enumerate(near_chips(d)):
            if d or way == 0:
                come(near.at[chip, rows[way]], nir.at[2 * d + way])

    eye = lax.broadcasted_iota(jnp.int32, (B, B), 0) == lax.broadcasted_iota(jnp.int32, (B, B), 1)
    three = range(3)

    def known(k):
        done = slice(0, k * B)
        xp = slab[at(k), :]
        if k:
            xp = xp - product([ls[s, at(k), done] for s in three], [xs[s, done, :] for s in three], False)
        return xp

    def solve(k, xp, inverse):
        solved = product(inverse, split(xp), False)
        x[at(k), :] = solved * math.sqrt(ROWS)
        if k < blocks - 1:
            solved = split(solved)
            for s in three:
                xs[s, at(k), :] = solved[s]

    def hand_over(ks):
        @pl.when(c < cuts - 1)
        def _():
            for k in ks:
                rows_out(2 * k).start()
                rows_out(2 * k + 1).start()

    for k in range(blocks):
        done = slice(0, k * B)
        top = WAIT + 1 if k < WAIT else blocks
        rest = slice((k + 1) * B, top * B)
        if k == WAIT:
            far_finish()
            far_complete()
        if k == LAG:
            for o in range(1, COL):
                rows = pl.ds(pl.multiple_of(lax.rem(me + COL - o, COL) * HALF, HALF), HALF)
                come(slab.at[rows], alr.at[o])
        if k:
            before = (WAIT + 1 if k <= WAIT else blocks) * B
            column = split(product(split(cs[k * B : before, :]), li))
            for s in three:
                ls[s, k * B : before, at(k - 1)] = column[s]
        if k == WAIT:
            low = slice((WAIT + 1) * B, K)
            for j in range(WAIT):
                early = slice(0, j * B)
                column = jnp.concatenate([gram_block(i, j) for i in range(WAIT + 1, blocks)], axis=0)
                if j:
                    column = column - product([ls[s, low, early] for s in three], [ls[s, at(j), early] for s in three])
                column = split(product(split(column), [lis[s, j] for s in three]))
                for s in three:
                    ls[s, low, at(j)] = column[s]
        if k:
            lk = [ls[s, at(k), done] for s in three]
        if k == LAG:
            for j in range(k):
                solve(j, known(j), [lis[s, j] for s in three])
        if k >= LAG:
            xp = known(k)
        if k < blocks - 1:
            later = gram_block(k + 1, k + 1)
            if k:
                taken = product([ls[s, rest, done] for s in three], lk)
                for i in range(k + 1, top):
                    cs[at(i), :] = gram_block(i, k) - taken[at(i - k - 1), :]
            else:
                for i in range(1, top):
                    cs[at(i), :] = gram_block(i, 0)
            if k:
                ln = [ls[s, at(k + 1), done] for s in three]
                later = later - product(ln, ln)
        if k:
            eliminate(d, inv, one)
        inverse = inv[...]
        li = split(inverse)
        if k < blocks - 1:
            l1 = split(product(split(cs[at(k + 1), :]), li))
            d = later - product(l1, l1)
        if k >= LAG:
            solve(k, xp, li)
        else:
            for s in three:
                lis[s, k] = li[s]
        diagonal = jnp.sum(jnp.where(eye, inverse, 0.0), axis=0, keepdims=True)
        piv[k : k + 1, :] = -jnp.log(diagonal) - 0.5 * math.log(ROWS)
        if k >= LAG:
            hand_over(range(k + 1) if k == LAG else (k,))

    give = []
    for o in range(1, cuts):
        s = remote(piv, allp.at[c], vs.at[o], vr.at[o], {"cuts": lax.rem(c + o, cuts), "col": me})
        s.start()
        give.append(s)
    allp[c] = piv[...]
    for o in range(1, cuts):
        come(allp.at[lax.rem(c + cuts - o, cuts)], vr.at[o])
    expo = tree([allp[o] for o in range(cuts)]) / (SLICES * cuts)
    means = means_of(expo)
    here = lax.broadcasted_iota(jnp.int32, (K // B, B), 0) == z
    for value, out in ((expo, exponents), (means, running)):
        line = jnp.sum(jnp.where(here, value, 0.0), axis=0, keepdims=True)
        out[...] = jnp.where(h == 0, line[:, :HALF], line[:, HALF:])

    @pl.when(c > 0)
    def _():
        for j in range(COL):
            come(handed.at[:, pl.ds(j * B, B)], xrs.at[j])

    @pl.when(c < cuts - 1)
    def _():
        for i in range(COL):
            rows_out(i).wait_send()

    @pl.when(z == 0)
    def _():
        for o in range(1, COL):
            first_out(o).wait_send()

    for way in range(2):
        for o in range(4):
            if o:
                far_out(way, o).wait_send()
            far_inside(way, o).wait_send()
    for i in range(4):
        if i < 3:
            across_out(i).wait_send()
        across_inside(i).wait_send()
    for s in sends + give:
        s.wait_send()


def local(cuts, levels, start_basis):
    start = start_basis[0]
    dma = pltpu.SemaphoreType.DMA
    handed, exponents, running = pl.pallas_call(
        functools.partial(sweep_kernel, cuts),
        out_shape=(
            jax.ShapeDtypeStruct((HALF, ROWS), f32),
            jax.ShapeDtypeStruct((1, HALF), f32),
            jax.ShapeDtypeStruct((1, HALF), f32),
        ),
        in_specs=[VMEM] * 2,
        out_specs=(VMEM,) * 3,
        scratch_shapes=[
            pltpu.VMEM((HALF, ROWS), f32),
            pltpu.VMEM((5, B, SITES), f32),
            pltpu.VMEM((B, BANDS), f32),
            pltpu.VMEM((HALF, BANDS), f32),
            pltpu.VMEM((B, B), f32),
            pltpu.VMEM((CHIPS, B, 3 * B), f32),
            pltpu.VMEM((CHIPS, B, B), f32),
            pltpu.VMEM((CHIPS // 2, B, B), f32),
            pltpu.VMEM((K, B), f32),
            pltpu.VMEM((K, B), f32),
            pltpu.VMEM((K // B, B), f32),
            pltpu.VMEM((cuts, K // B, B), f32),
            pltpu.VMEM((3, K, K), bf16),
            pltpu.VMEM((3, K, B), bf16),
            pltpu.VMEM((K, B), f32),
            pltpu.VMEM((3, max(LAG, 1), B, B), bf16),
            pltpu.VMEM((B, B), f32),
            pltpu.VMEM((8, B), f32),
            dma((5,)), dma((10,)), dma((8,)), dma((8,)), dma((3,)), dma((3,)), dma((COL,)), dma((2,)),
            dma((10,)), dma((10,)), dma((10,)), dma((10,)),
            dma((CHIPS,)), dma((CHIPS,)), dma((CHIPS,)), dma((CHIPS,)), dma((3,)), dma((3,)), dma((4,)), dma((4,)),
            dma((COL,)), dma((COL,)), dma((COL,)), dma((COL,)), dma((cuts,)), dma((cuts,)),
        ],
        compiler_params=pltpu.CompilerParams(
            collective_id=1, has_side_effects=True, vmem_limit_bytes=48 << 20
        ),
        name="sweep",
    )(levels, start)
    return exponents[0], running[0], handed[None]


def solution(mesh):
    in_specs = (P("cuts", None), P("cuts", "col", None))
    out_specs = (P("col"), P("col"), P("cuts", "col", None))
    return jax.shard_map(
        functools.partial(local, mesh.shape["cuts"]), mesh=mesh, in_specs=in_specs, out_specs=out_specs, check_vma=False
    )
```

time: 120 us -> 108 us (0.900)
  Pallas kernels: 115 us -> 104 us
    pallas_call x2 -> x1, Pallas kernels: 115 us -> 104 us  [local(): pl.pallas_call(functools.partial(sweep_kernel, cuts), out_shape=(jax.Shap...]
    unnamed x9 -> x7, local copies, waits for them, and re-layouts: 4.59 us -> 3.55 us
where the time goes in v3:
time: 108 us
  Pallas kernels  104 us (96%)
  local copies, waits for them, and re-layouts  3.55 us (3%)
    pallas_call x1, Pallas kernels, local(): pl.pallas_call(functools.partial(sweep_kernel, cuts), out_shape=(jax.Shap...  104 us
    unnamed x7, local copies, waits for them, and re-layouts  3.55 us

profile of v3, /device:TPU:1, one launch (start us, length us, event | category | flops | bytes accessed | tf_op | source)
XLA Modules:
  0.0 107.8 jit_solution(8150510675245010142)
XLA Ops:
  0.6 0.0 copy-start
  0.6 1.0 copy-done
  1.7 0.0 copy-start.1
  1.7 0.7 copy-done.1
  2.4 103.6 %sweep.1 = (f32[64,2048]{1,0:T(8,128)S(1)}, f32[1,64]{1,0:T(1,128)S(1)}, f32[1,64]{1,0:T(1,128)S(1)}) custom-call(s32[2,1024]{1,0:T(2,128)S(1)} %copy-done.1, f32[64,2048]{1,0:T(8,128)S(1)} %bitcast.4), custom_call_target="tpu_custom_call" | custom-call | tf_op jit(solution)/shard_map/sweep/pallas_call | solution.py:554
  106.0 0.5 copy.8
  106.5 0.5 copy.9
  107.0 0.8 copy.10
Async XLA Ops:
  0.6 1.0 copy-start
  1.7 0.7 copy-start.1

commit v4 on v3

--- a/solution.py
+++ b/solution.py
@@ -140,9 +140,9 @@
 
 
 def sweep_kernel(
-    cuts, lev, start, handed, exponents, running,
-    prop, gat, part, other, first, near, far, across, slab, x, piv, allp, ls, xs, cs, lis, inv, ones,
-    gs, gr, fs, g2r, ps, pr, d0s, d0r, ns, nr, nis, nir, f3s, f3r, f3is, f3ir, f4s, f4r, f4is, f4ir,
+    cuts, levels, basis, handed, exponents, running,
+    lev, start, ins, prop, gat, part, other, near, far, across, slab, x, piv, allp, ls, xs, cs, lis, inv, ones,
+    gs, gr, fs, g2r, ps, pr, ns, nr, nis, nir, f3s, f3r, f3is, f3ir, f4s, f4r, f4is, f4ir,
     als, alr, xss, xrs, vs, vr,
 ):
     me = lax.axis_index("col")
@@ -156,6 +156,9 @@
     my_rows = pl.ds(pl.multiple_of(me * HALF, HALF), HALF)
     blocks = K // B
     sends = []
+    loads = [pltpu.make_async_copy(levels, lev, ins.at[0]), pltpu.make_async_copy(basis, start, ins.at[1])]
+    for load in loads:
+        load.start()
 
     barrier = pltpu.get_barrier_semaphore()
     for o in range(1, COL):
@@ -170,6 +173,8 @@
         for i in range(COL):
             pl.semaphore_signal(barrier, inc=1, device_id={"cuts": c - 1, "col": i}, device_id_type=MESH)
 
+    for load in loads:
+        load.wait()
     upper = start[:, :SITES]
     lower = start[:, SITES:]
     for n in range(SLICES):
@@ -363,18 +368,7 @@
     come(gat.at[0, theirs], gr.at[1 - h])
     make(0)
 
-    def first_out(o):
-        ref = first.at[mine]
-        return remote(ref, ref, d0s.at[o], d0r.at[h], {"col": lax.rem(me + o, COL)})
-
-    diagonal_half = pair_sum(0, 0, 1)
-    near[z, mine, 0:B] = diagonal_half
-
-    @pl.when(z == 0)
-    def _():
-        first[mine, :] = diagonal_half
-        for o in range(1, COL):
-            first_out(o).start()
+    near[z, mine, 0:B] = pair_sum(0, 0, 1)
 
     arrived(1, h)
     arrived(3, h)
@@ -391,19 +385,6 @@
     near_step(2)
     second_hop(2)
 
-    @pl.when(z == 0)
-    def _():
-        come(first.at[theirs], d0r.at[1 - h])
-
-    @pl.when(z > 0)
-    def _():
-        for s in range(2):
-            come(first.at[pl.ds(s * HALF, HALF)], d0r.at[s])
-
-    ones[...] = jnp.ones_like(ones)
-    one = ones[...]
-    eliminate(first[...], inv, one)
-
     near_come(2)
     near_step(3)
     second_hop(3)
@@ -417,6 +398,9 @@
         for way, chip in enumerate(near_chips(d)):
             if d or way == 0:
                 come(near.at[chip, rows[way]], nir.at[2 * d + way])
+
+    ones[...] = jnp.ones_like(ones)
+    one = ones[...]
 
     eye = lax.broadcasted_iota(jnp.int32, (B, B), 0) == lax.broadcasted_iota(jnp.int32, (B, B), 1)
     three = range(3)
@@ -488,8 +472,9 @@
             if k:
                 ln = [ls[s, at(k + 1), done] for s in three]
                 later = later - product(ln, ln)
-        if k:
-            eliminate(d, inv, one)
+        if k == 0:
+            d = gram_block(0, 0)
+        eliminate(d, inv, one)
         inverse = inv[...]
         li = split(inverse)
         if k < blocks - 1:
@@ -530,11 +515,6 @@
         for i in range(COL):
             rows_out(i).wait_send()
 
-    @pl.when(z == 0)
-    def _():
-        for o in range(1, COL):
-            first_out(o).wait_send()
-
     for way in range(2):
         for o in range(4):
             if o:
@@ -558,14 +538,16 @@
             jax.ShapeDtypeStruct((1, HALF), f32),
             jax.ShapeDtypeStruct((1, HALF), f32),
         ),
-        in_specs=[VMEM] * 2,
+        in_specs=[pl.BlockSpec(memory_space=pl.ANY)] * 2,
         out_specs=(VMEM,) * 3,
         scratch_shapes=[
+            pltpu.VMEM((SLICES, SITES), jnp.int32),
+            pltpu.VMEM((HALF, ROWS), f32),
+            dma((2,)),
             pltpu.VMEM((HALF, ROWS), f32),
             pltpu.VMEM((5, B, SITES), f32),
             pltpu.VMEM((B, BANDS), f32),
             pltpu.VMEM((HALF, BANDS), f32),
-            pltpu.VMEM((B, B), f32),
             pltpu.VMEM((CHIPS, B, 3 * B), f32),
             pltpu.VMEM((CHIPS, B, B), f32),
             pltpu.VMEM((CHIPS // 2, B, B), f32),
@@ -579,7 +561,7 @@
             pltpu.VMEM((3, max(LAG, 1), B, B), bf16),
             pltpu.VMEM((B, B), f32),
             pltpu.VMEM((8, B), f32),
-            dma((5,)), dma((10,)), dma((8,)), dma((8,)), dma((3,)), dma((3,)), dma((COL,)), dma((2,)),
+            dma((5,)), dma((10,)), dma((8,)), dma((8,)), dma((3,)), dma((3,)),
             dma((10,)), dma((10,)), dma((10,)), dma((10,)),
             dma((CHIPS,)), dma((CHIPS,)), dma((CHIPS,)), dma((CHIPS,)), dma((3,)), dma((3,)), dma((4,)), dma((4,)),
             dma((COL,)), dma((COL,)), dma((COL,)), dma((COL,)), dma((cuts,)), dma((cuts,)),

time: 108 us -> 105 us (0.972)
  Pallas kernels: 104 us -> 99.6 us
    pallas_call x1, Pallas kernels: 104 us -> 99.6 us  [local(): pl.pallas_call(functools.partial(sweep_kernel, cuts), out_shape=(jax.Shap...]
where the time goes in v4:
time: 105 us; the launch traced here: 104 us
  Pallas kernels  99.6 us (95%)
  local copies, waits for them, and re-layouts  3.55 us (3%)
    pallas_call x1, Pallas kernels, local(): pl.pallas_call(functools.partial(sweep_kernel, cuts), out_shape=(jax.Shap...  99.6 us
    unnamed x7, local copies, waits for them, and re-layouts  3.55 us

profile of v4, /device:TPU:1, one launch (start us, length us, event | category | flops | bytes accessed | tf_op | source)
XLA Modules:
  0.0 103.8 jit_solution(14942829078746446630)
XLA Ops:
  0.6 0.0 copy-start
  0.6 1.0 copy-done
  1.7 0.0 copy-start.1
  1.7 0.7 copy-done.1
  2.4 99.6 %sweep.1 = (f32[64,2048]{1,0:T(8,128)S(1)}, f32[1,64]{1,0:T(1,128)S(1)}, f32[1,64]{1,0:T(1,128)S(1)}) custom-call(s32[2,1024]{1,0:T(2,128)S(1)} %copy-done.1, f32[64,2048]{1,0:T(8,128)S(1)} %bitcast.4), custom_call_target="tpu_custom_call" | custom-call | tf_op jit(solution)/shard_map/sweep/pallas_call | solution.py:534
  102.0 0.5 copy.8
  102.5 0.5 copy.9
  103.0 0.8 copy.10
Async XLA Ops:
  0.6 1.0 %copy-start = (f32[1,64,2048]{2,1,0:T(8,128)S(1)}, f32[1,64,2048]{2,1,0:T(8,128)}, u32[]{:S(2)}) copy-start(f32[1,64,2048]{2,1,0:T(8,128)} %param.3) | copy-start | bytes 1572868
  1.7 0.7 copy-start.1

commit v5 on v4

--- a/solution.py
+++ b/solution.py
@@ -163,10 +163,16 @@
     barrier = pltpu.get_barrier_semaphore()
     for o in range(1, COL):
         pl.semaphore_signal(barrier, inc=1, device_id={"col": lax.rem(me + o, COL)}, device_id_type=MESH)
-    for o in range(1, cuts):
-        pl.semaphore_signal(
-            barrier, inc=1, device_id={"cuts": lax.rem(c + o, cuts), "col": me}, device_id_type=MESH
-        )
+    inner = min(8, cuts)
+    outer = cuts // inner
+    cx, cy = c // inner, c % inner
+    stages = (
+        (inner, 0, cy, lambda o: cx * inner + lax.rem(cy + o, inner)),
+        (outer, inner, cx, lambda o: lax.rem(cx + o, outer) * inner + cy),
+    )
+    for count, _, _, mate in stages:
+        for o in range(1, count):
+            pl.semaphore_signal(barrier, inc=1, device_id={"cuts": mate(o), "col": me}, device_id_type=MESH)
 
     @pl.when(c > 0)
     def _():
@@ -187,7 +193,7 @@
     def _():
         handed[...] = start[...]
 
-    everyone = COL - 1 + cuts - 1
+    everyone = COL - 1 + inner - 1 + outer - 1
     pl.semaphore_wait(barrier, jnp.where(c < cuts - 1, everyone + COL, everyone))
 
     their_half = pl.ds(pl.multiple_of((1 - h) * SITES, SITES), SITES)
@@ -491,14 +497,18 @@
             hand_over(range(k + 1) if k == LAG else (k,))
 
     give = []
-    for o in range(1, cuts):
-        s = remote(piv, allp.at[c], vs.at[o], vr.at[o], {"cuts": lax.rem(c + o, cuts), "col": me})
-        s.start()
-        give.append(s)
-    allp[c] = piv[...]
-    for o in range(1, cuts):
-        come(allp.at[lax.rem(c + cuts - o, cuts)], vr.at[o])
-    expo = tree([allp[o] for o in range(cuts)]) / (SLICES * cuts)
+    total = piv[...]
+    for count, base, position, mate in stages:
+        allp[base + position] = total
+        ref = allp.at[base + position]
+        for o in range(1, count):
+            out = remote(ref, ref, vs.at[base + o], vr.at[base + o], {"cuts": mate(o), "col": me})
+            out.start()
+            give.append(out)
+        for o in range(1, count):
+            come(allp.at[base + lax.rem(position + count - o, count)], vr.at[base + o])
+        total = tree([allp[base + i] for i in range(count)])
+    expo = total / (SLICES * cuts)
     means = means_of(expo)
     here = lax.broadcasted_iota(jnp.int32, (K // B, B), 0) == z
     for value, out in ((expo, exponents), (means, running)):
@@ -554,7 +564,7 @@
             pltpu.VMEM((K, B), f32),
             pltpu.VMEM((K, B), f32),
             pltpu.VMEM((K // B, B), f32),
-            pltpu.VMEM((cuts, K // B, B), f32),
+            pltpu.VMEM((cuts + 1, K // B, B), f32),
             pltpu.VMEM((3, K, K), bf16),
             pltpu.VMEM((3, K, B), bf16),
             pltpu.VMEM((K, B), f32),
@@ -564,7 +574,7 @@
             dma((5,)), dma((10,)), dma((8,)), dma((8,)), dma((3,)), dma((3,)),
             dma((10,)), dma((10,)), dma((10,)), dma((10,)),
             dma((CHIPS,)), dma((CHIPS,)), dma((CHIPS,)), dma((CHIPS,)), dma((3,)), dma((3,)), dma((4,)), dma((4,)),
-            dma((COL,)), dma((COL,)), dma((COL,)), dma((COL,)), dma((cuts,)), dma((cuts,)),
+            dma((COL,)), dma((COL,)), dma((COL,)), dma((COL,)), dma((cuts + 1,)), dma((cuts + 1,)),
         ],
         compiler_params=pltpu.CompilerParams(
             collective_id=1, has_side_effects=True, vmem_limit_bytes=48 << 20

time: 105 us -> 106 us (level)
  the two profiles are of different devices: /device:TPU:1 before, /device:TPU:8 now
where the time goes in v5:
time: 106 us; the launch traced here: 105 us
  Pallas kernels  101 us (95%)
  local copies, waits for them, and re-layouts  3.55 us (3%)
    pallas_call x1, Pallas kernels, local(): pl.pallas_call(functools.partial(sweep_kernel, cuts), out_shape=(jax.Shap...  101 us
    unnamed x7, local copies, waits for them, and re-layouts  3.55 us

profile of v5, /device:TPU:8, one launch (start us, length us, event | category | flops | bytes accessed | tf_op | source)
XLA Modules:
  0.0 105.4 jit_solution(15216177862104788395)
XLA Ops:
  0.6 0.0 copy-start
  0.6 1.0 copy-done
  1.7 0.0 copy-start.1
  1.7 0.7 copy-done.1
  2.4 101.2 %sweep.1 = (f32[64,2048]{1,0:T(8,128)S(1)}, f32[1,64]{1,0:T(1,128)S(1)}, f32[1,64]{1,0:T(1,128)S(1)}) custom-call(s32[2,1024]{1,0:T(2,128)S(1)} %copy-done.1, f32[64,2048]{1,0:T(8,128)S(1)} %bitcast.4), custom_call_target="tpu_custom_call" | custom-call | tf_op jit(solution)/shard_map/sweep/pallas_call | solution.py:544
  103.6 0.5 copy.8
  104.1 0.5 copy.9
  104.6 0.8 copy.10
Async XLA Ops:
  0.6 1.0 copy-start
  1.7 0.7 copy-start.1
